TPU v7x, 128 devices: a whole 4x4x4 slice. The times are simulated.
128 devices in a mesh: lat: 4 (over y_hi, core), lon: 32 (over y_lo, z, x).
Axes of the slice: x: 4, y: 4 (y_hi: 2, y_lo: 2; y = y_hi * 2 + y_lo), z: 4, core: 2. Of those that a mesh axis runs over, the one named last changes fastest.
Arguments:
- atmosphere: float32 [4, 24, 384, 512], P(None, 'lat', 'lon'), may hold values from -125 to 125
- norm_gain: float32 [2, 512], replicated, may hold values from 0.5 to 1.5
- qkv_weight: bfloat16 [2, 512, 1536], replicated, may hold values from -0.25 to 0.25
- out_weight: bfloat16 [2, 512, 512], replicated, may hold values from -0.25 to 0.25
- position_bias: float32 [2, 16, 759], replicated, may hold values from -3 to 225
Outputs:
- mixed_field: float32 [4, 24, 384, 512], P(None, 'lat', 'lon')
All inputs are finite; a program needn't handle non-finite values.
Results may differ from a plain program's by a relative error of at most 0.001.
Values sent between devices are 32-bit elements; how exact they have to be, the bound alone decides.
A program may use at most 128 MiB of HBM per device.

v0:
```python
import functools
import math

import jax
import jax.numpy as jnp
import ml_dtypes
import numpy as np
from jax import lax
from jax.experimental import pallas as pl
from jax.experimental.pallas import tpu as pltpu
from jax.sharding import PartitionSpec as P

D = 512
HEADS = 16
HEAD_DIM = 32
WIN = 144
QUAD = 40
ROWS = 4 * QUAD
HALF = 18
GROUP = 8
TILES = GROUP + 1
TABLE = 759
EPSILON = 1e-05
LOG2E = math.log2(math.e)
SCORE_SCALE = LOG2E * HEAD_DIM ** (-0.5)
EXCLUDED = -1e30
TW, TE, BW, BE = 0, 1, 2, 3
MESH = pl.DeviceIdType.MESH


def token_places(shifted):
    places = np.full(ROWS, -1)
    for lat in range(2):
        for lon in range(2):
            for lev in range(2):
                for r in range(3):
                    for c in range(6):
                        a, l, o = lat * 3 + r, lev, lon * 6 + c
                        if shifted:
                            a, l, o = (a + 3) % 6, 1 - l, (o + 6) % 12
                        row = (lat * 2 + lon) * QUAD + lev * HALF + r * 6 + c
                        places[row] = a * 24 + l * 12 + o
    return places


def constants():
    bf16 = ml_dtypes.bfloat16
    perm_in = np.zeros((2, WIN, ROWS), np.float32)
    perm_out = np.zeros((2, ROWS, 256), np.float32)
    for block in range(2):
        for row, token in enumerate(token_places(block == 1)):
            if token >= 0:
                perm_in[block, token, row] = 1
                perm_out[block, row, token] = 1
    token = np.arange(WIN)
    row, level, col = token // 24, token // 12 % 2, token % 12

    def offsets(query):
        delta = lambda x: x[:, None] - x[query][None, :]
        return ((delta(level) + 1) * 11 + delta(row) + 5) * 23 + delta(col) + 11

    lane = np.arange(128)
    queries = [lane, 128 + lane % 16]
    index = np.stack([offsets(q) for q in queries]).astype(np.int32)
    slot_lat, slot_level = 1 - row // 3, 1 - level
    regions = [
        slot_level,
        np.where(slot_lat == 1, 0, 1 + slot_level),
        np.where(slot_lat == 0, slot_level, 2),
    ]
    masks = np.stack(
        [
            np.stack([np.where(g[:, None] == g[q][None, :], 0, EXCLUDED) for q in queries])
            for g in regions
        ]
    ).astype(np.float32)
    head_lanes = (np.arange(256)[None, :] // HEAD_DIM == np.arange(16)[:, None]).astype(bf16)
    rest_lanes = (np.arange(256)[:, None] // HEAD_DIM == lane[None, :] // 16).astype(np.float32)
    fold = ((lane[:, None] % 16) == lane[None, :]).astype(bf16)
    return (
        perm_in.astype(bf16),
        perm_out.astype(bf16),
        np.eye(256).astype(bf16),
        head_lanes,
        rest_lanes,
        fold,
        index,
        masks,
    )


CONSTANTS = constants()
TOUCHED = [
    [sorted(set((CONSTANTS[6][part, 8 * i : 8 * i + 8] >> 7).reshape(-1).tolist())) for i in range(18)]
    for part in range(2)
]


def nt_dot(a, b):
    return lax.dot_general(a, b, (((1,), (1,)), ((), ())), preferred_element_type=jnp.float32)


def dot(a, b):
    return jnp.dot(a, b, preferred_element_type=jnp.float32)


def looked_up(table_ref, head, lanes, tiles, touched):
    found = None
    for tile in touched:
        source = table_ref[head, :, 128 * tile : 128 * tile + 128]
        picked = jnp.take_along_axis(source, lanes, axis=1)
        found = picked if found is None else jnp.where(tiles == tile, picked, found)
    return found


def expand_bias(table_ref, index_ref, stores):
    def one_head(head, carry):
        group = head // GROUP
        place = head - group * GROUP
        rest_from = place * 16
        lane = lax.broadcasted_iota(jnp.int32, (8, 128), 1)
        for strip in range(18):
            rows = slice(8 * strip, 8 * strip + 8)
            for part in range(2):
                where_found = index_ref[part, rows, :]
                values = looked_up(
                    table_ref, head, where_found & 127, where_found >> 7, TOUCHED[part][strip]
                )
                if part == 0:
                    for store in stores:
                        store(group * TILES + place, rows, 0, values, None)
                else:
                    for store in stores:
                        store(group * TILES + GROUP, rows, 1, values, lane >= rest_from)
        return carry

    lax.fori_loop(0, HEADS, one_head, 0)


def attend(state, gain, perm_in, perm_out, qkv_ref, out_ref, bias_at, head_ref, rest_lanes, fold, eye, mixed_ref):
    center = state - jnp.mean(state, axis=-1, keepdims=True)
    spread = jnp.mean(center * center, axis=-1, keepdims=True)
    normed = (center * lax.rsqrt(spread + EPSILON) * gain).astype(jnp.bfloat16)
    normed = dot(perm_in, normed).astype(jnp.bfloat16)
    for group in range(HEADS // GROUP):
        lanes = slice(group * 256, group * 256 + 256)
        queries, keys, values = (
            dot(normed, qkv_ref[:, D * part + group * 256 : D * part + group * 256 + 256]).astype(
                jnp.bfloat16
            )
            for part in range(3)
        )
        values = nt_dot(eye, values).astype(jnp.bfloat16)
        rest = []
        for tile in range(TILES):
            if tile < GROUP:
                chosen = head_ref[tile : tile + 1, :]
                masked = queries[:128] * chosen
                rest.append(queries[128:] * chosen)
            else:
                masked = jnp.concatenate(rest, axis=0)
            scores = nt_dot(keys, masked) * SCORE_SCALE + bias_at(group * TILES + tile)
            exponents = jnp.exp2(scores - jnp.max(scores, axis=0, keepdims=True))
            scale = 1.0 / jnp.sum(exponents, axis=0, keepdims=True)
            exponents = exponents.astype(jnp.bfloat16)
            if tile < GROUP:
                here = slice(tile * HEAD_DIM, tile * HEAD_DIM + HEAD_DIM)
                mixed_ref[group * 256 + tile * HEAD_DIM : group * 256 + (tile + 1) * HEAD_DIM, :128] = (
                    dot(values[here], exponents) * scale
                ).astype(jnp.bfloat16)
            else:
                mixed = (dot(values, exponents) * scale * rest_lanes).astype(jnp.bfloat16)
                mixed_ref[lanes, 128:] = dot(mixed, fold).astype(jnp.bfloat16)
    mixed = nt_dot(perm_out, mixed_ref[...]).astype(jnp.bfloat16)
    return state + dot(mixed, out_ref[...])


def kernel(
    lat_count,
    lon_count,
    x_ref,
    gain_ref,
    qkv_ref,
    out_ref,
    table_ref,
    perm_in_ref,
    perm_out_ref,
    eye_ref,
    head_ref,
    rest_ref,
    fold_ref,
    index_ref,
    mask_ref,
    result_ref,
    tables,
    bias,
    plain,
    sends,
    frame,
    backs,
    home,
    mixed_ref,
    send_sem,
    recv_sem,
    back_send_sem,
    back_recv_sem,
    local_sem,
):
    i = lax.axis_index("lat")
    j = lax.axis_index("lon")
    east = lax.rem(j + 1, lon_count)
    west = lax.rem(j + lon_count - 1, lon_count)
    inner = lat_count - 1
    is_first = (inner - i) // inner
    is_last = i // inner

    barrier = pltpu.get_barrier_semaphore()

    def greet(lat, lon):
        pl.semaphore_signal(barrier, inc=1, device_id=(lat, lon), device_id_type=MESH)

    greet(i, west)
    greet(i, east)

    @pl.when(i > 0)
    def _():
        greet(i - 1, j)
        greet(i - 1, west)

    @pl.when(i < inner)
    def _():
        greet(i + 1, j)
        greet(i + 1, east)

    for block in range(2):
        for head in range(HEADS):
            tables[block, head, :, :TABLE] = jnp.broadcast_to(
                table_ref[block, head : head + 1, :] * LOG2E, (8, TABLE)
            )

    def put(which, added):
        def store(slot, rows, part, values, keep):
            if added is not None:
                values = values + added(part, rows)
            if keep is not None:
                values = jnp.where(keep, values, bias[which, slot, rows, :])
            bias[which, slot, rows, :] = values

        return store

    last = is_last.astype(jnp.float32)
    first = is_first.astype(jnp.float32)
    expand_bias(tables.at[0], index_ref, [put(0, None)])

    def window(block, which, state):
        return attend(
            state,
            gain_ref[block : block + 1, :],
            perm_in_ref[block],
            perm_out_ref[block],
            qkv_ref.at[block],
            out_ref.at[block],
            lambda slot: bias[which, slot],
            head_ref,
            rest_ref[...],
            fold_ref[...],
            eye_ref[...],
            mixed_ref,
        )

    def plain_window(w, carry):
        plain[w] = window(0, 0, x_ref[w])
        return carry

    lax.fori_loop(0, 2, plain_window, 0)

    low = lax.broadcasted_iota(jnp.int32, (QUAD, D), 0) < HALF
    for quad in range(4):
        rows = slice(quad * QUAD, quad * QUAD + QUAD)
        even, odd = plain[0, rows, :], plain[1, rows, :]
        sends[0, quad] = jnp.where(low, odd, even)
        sends[1, quad] = jnp.where(low, even, odd)

    pl.semaphore_wait(barrier, 2 + 2 * (1 - is_first) + 2 * (1 - is_last))

    def remote(src, src_which, src_quad, dst, which, quad, lat, lon, send, recv):
        return pltpu.make_async_remote_copy(
            src_ref=src.at[src_which, src_quad],
            dst_ref=dst.at[which, quad],
            send_sem=send.at[src_which * 4 + src_quad],
            recv_sem=recv.at[which * 4 + quad],
            device_id=(lat, lon),
            device_id_type=MESH,
        )

    def local(src, src_which, src_quad, dst, which, quad):
        dst[which, quad] = src[src_which, src_quad]

    up, down = i - 1 + is_first, i + 1 - is_last

    out_ref_args = (sends, frame, send_sem, recv_sem)

    def outward(which, quad, to_which, to_quad, lat, lon):
        return remote(sends, which, quad, frame, to_which, to_quad, lat, lon, send_sem, recv_sem)

    def always_out():
        return [
            outward(0, TW, is_first, TW + is_first * (BW - TW), up, west),
            outward(1, BE, 1 - is_last, BE - is_last * (BE - TE), down, east),
            outward(0, BW, 0, BW, i, west),
            outward(1, TE, 1, TE, i, east),
        ]

    def up_out():
        return outward(0, TE, 0, TE, i - 1, j)

    def down_out():
        return outward(1, BW, 1, BW, i + 1, j)

    for copy in always_out():
        copy.start()

    @pl.when(i > 0)
    def _():
        up_out().start()

    @pl.when(i == 0)
    def _():
        local(sends, 0, TE, frame, 1, BE)

    @pl.when(i < inner)
    def _():
        down_out().start()

    @pl.when(i == inner)
    def _():
        local(sends, 1, BW, frame, 0, TW)

    local(sends, 0, BE, frame, 0, BE)
    local(sends, 1, TW, frame, 1, TW)

    expand_bias(
        tables.at[1],
        index_ref,
        [
            put(1, lambda part, rows: mask_ref[1, part, rows, :] * last),
            put(
                2,
                lambda part, rows: mask_ref[0, part, rows, :] * (1 - first)
                + mask_ref[2, part, rows, :] * first,
            ),
        ],
    )

    def arrived(ref, sem, which, quad):
        pltpu.make_async_copy(ref.at[which, quad], ref.at[which, quad], sem.at[which * 4 + quad]).wait()

    def backward(which, quad, to_which, to_quad, lat, lon):
        return remote(
            backs, which, quad, home, to_which, to_quad, lat, lon, back_send_sem, back_recv_sem
        )

    arrived(frame, recv_sem, 0, BW)
    arrived(frame, recv_sem, 0, TE)

    @pl.when(i < inner)
    def _():
        arrived(frame, recv_sem, 0, TW)

    backs[0] = window(1, 1, frame[0].reshape(ROWS, D)).reshape(4, QUAD, D)

    def first_back():
        return [
            backward(0, TE, is_last, TE + is_last * (BE - TE), down, j - is_last * (j - west)),
            backward(0, BW, 0, BW, i, east),
        ]

    def corner_back():
        return backward(0, TW, 0, TW, i + 1, east)

    for copy in first_back():
        copy.start()

    @pl.when(i < inner)
    def _():
        corner_back().start()

    @pl.when(i == inner)
    def _():
        local(backs, 0, TW, home, 1, BW)

    local(backs, 0, BE, home, 0, BE)

    arrived(frame, recv_sem, 1, TE)
    arrived(frame, recv_sem, 1, BW)

    @pl.when(i > 0)
    def _():
        arrived(frame, recv_sem, 1, BE)

    backs[1] = window(1, 2, frame[1].reshape(ROWS, D)).reshape(4, QUAD, D)

    def second_back():
        return [
            backward(1, BW, 1 - is_first, BW - is_first * (BW - TW), up, j - is_first * (j - east)),
            backward(1, TE, 1, TE, i, west),
        ]

    def other_corner_back():
        return backward(1, BE, 1, BE, i - 1, west)

    for copy in second_back():
        copy.start()

    @pl.when(i > 0)
    def _():
        other_corner_back().start()

    @pl.when(i == 0)
    def _():
        local(backs, 1, BE, home, 0, TE)

    local(backs, 1, TW, home, 1, TW)

    for which, quad in ((0, TW), (0, BW), (1, TE), (1, BE)):
        arrived(home, back_recv_sem, which, quad)

    @pl.when(i > 0)
    def _():
        arrived(home, back_recv_sem, 0, TE)

    @pl.when(i < inner)
    def _():
        arrived(home, back_recv_sem, 1, BW)

    for quad in range(4):
        rows = slice(quad * QUAD, quad * QUAD + QUAD)
        mid, outer = home[0, quad], home[1, quad]
        result_ref[0, rows, :] = jnp.where(low, outer, mid)
        result_ref[1, rows, :] = jnp.where(low, mid, outer)

    for copy in always_out() + first_back() + second_back():
        copy.wait_send()

    @pl.when(i > 0)
    def _():
        up_out().wait_send()
        other_corner_back().wait_send()

    @pl.when(i < inner)
    def _():
        down_out().wait_send()
        corner_back().wait_send()


def shards(lat_count, lon_count, atmosphere, norm_gain, qkv_weight, out_weight, position_bias):
    x = atmosphere.reshape(2, 2, 2, 3, 2, 6, D).transpose(0, 2, 4, 1, 3, 5, 6)
    x = x.reshape(2, 4, 2 * HALF, D)
    x = jnp.pad(x, ((0, 0), (0, 0), (0, QUAD - 2 * HALF), (0, 0))).reshape(2, ROWS, D)
    operands = [x, norm_gain, qkv_weight, out_weight, position_bias]
    operands += [jnp.asarray(c) for c in CONSTANTS]
    buffer = pltpu.VMEM((2, 4, QUAD, D), jnp.float32)
    result = pl.pallas_call(
        functools.partial(kernel, lat_count, lon_count),
        out_shape=jax.ShapeDtypeStruct((2, ROWS, D), jnp.float32),
        in_specs=[pl.BlockSpec(memory_space=pltpu.VMEM)] * len(operands),
        out_specs=pl.BlockSpec(memory_space=pltpu.VMEM),
        scratch_shapes=[
            pltpu.VMEM((2, HEADS, 8, 768), jnp.float32),
            pltpu.VMEM((3, 2 * TILES, WIN, 128), jnp.float32),
            pltpu.VMEM((2, ROWS, D), jnp.float32),
            buffer,
            buffer,
            buffer,
            buffer,
            pltpu.VMEM((D, 256), jnp.bfloat16),
            pltpu.SemaphoreType.DMA((8,)),
            pltpu.SemaphoreType.DMA((8,)),
            pltpu.SemaphoreType.DMA((8,)),
            pltpu.SemaphoreType.DMA((8,)),
            pltpu.SemaphoreType.DMA((2,)),
        ],
        compiler_params=pltpu.CompilerParams(
            collective_id=0, has_side_effects=True, vmem_limit_bytes=48 * 1024 * 1024
        ),
    )(*operands)
    result = result.reshape(2, 4, QUAD, D)[:, :, : 2 * HALF]
    result = result.reshape(2, 2, 2, 2, 3, 6, D).transpose(0, 3, 1, 4, 2, 5, 6)
    return result.reshape(4, 6, 12, D)


def solution(mesh):
    in_specs = (P(None, "lat", "lon", None), P(), P(), P(), P())
    out_specs = P(None, "lat", "lon", None)
    body = functools.partial(shards, mesh.shape["lat"], mesh.shape["lon"])
    return jax.shard_map(body, mesh=mesh, in_specs=in_specs, out_specs=out_specs, check_vma=False)
```

profile of v0, /device:TPU:1, one launch (start us, length us, event | category | flops | bytes accessed | tf_op | source)
XLA Modules:
  0.0 44.7 jit_solution(5446726405328695238)
XLA Ops:
  0.0 0.0 copy-start.1
  0.0 0.0 copy-start.3
  0.0 0.0 copy-start.8
  0.0 0.0 copy-start.5
  0.0 0.0 copy-start.9
  0.0 0.0 copy-start.6
  0.0 0.0 copy-start.2
  0.1 0.0 copy-start.4
  0.1 0.0 copy-start.7
  0.1 0.0 copy-start
  0.1 0.0 copy-start.10
  0.1 1.7 %reshape.18 = f32[2,2,2,3,2,6,512]{6,1,0,5,4,3,2:T(2,128)S(1)} reshape(f32[4,6,12,512]{3,0,2,1:T(4,128)} %param.13) | data formatting | bytes 1179648 | tf_op jit(solution)/shard_map/reshape | solution.py:457
  1.8 0.3 copy.19
  2.1 0.1 copy.24
  2.3 0.0 copy-done.1
  2.3 0.0 copy-done.3
  2.3 0.0 copy-done.8
  2.3 0.0 copy-done.5
  2.3 0.0 copy-done.9
  2.3 0.0 copy-done.6
  2.3 0.0 copy-done.2
  2.3 0.0 copy-done.4
  2.3 0.0 copy-done.7
  2.4 0.0 copy-done
  2.4 0.0 copy-done.10
  2.4 40.2 %shard_map.127 = f32[2,160,512]{2,1,0:T(8,128)S(1)} custom-call(f32[2,160,512]{2,1,0:T(8,128)S(1)} %bitcast.13, f32[2,512]{1,0:T(2,128)S(1)} %copy-done.10, bf16[2,512,1536]{2,1,0:T(8,128)(2,1)} %qkv_ref.1, bf16[2,512,512]{2,1,0:T(8,128)(2,1)S(1)} %copy-done, f32[2,16,759]{2,1,0:T(8,128)S(1)} %copy-done.7, bf16[2,144,160]{2,1,0:T(8,128)(2,1)S(1)} %copy-done.4, ...), custom_call_target="tpu_custom_call" | custom-call | tf_op jit(solution)/shard_map/pallas_call | solution.py:463
  42.6 0.5 %copy.23 = f32[2,4,36,512]{3,0,2,1:T(2,128)S(1)} copy(f32[2,4,36,512]{3,2,1,0:T(8,128)S(1)} %bitcast.14) | data formatting | bytes 1179648
  43.1 0.3 copy.22
  43.4 1.3 %reshape.23 = f32[4,6,12,512]{3,0,2,1:T(4,128)} reshape(f32[2,2,2,3,2,6,512]{6,1,0,5,4,3,2:T(2,128)S(1)} %copy.22) | data formatting | bytes 1179648 | tf_op jit(solution)/shard_map/reshape | solution.py:489
  (1 shorter events, 0.0 us)
Async XLA Ops:
  0.0 2.3 %copy-start.1 = (f32[3,2,144,128]{3,2,1,0:T(8,128)S(1)}, f32[3,2,144,128]{3,2,1,0:T(8,128)}, u32[]{:S(2)}) copy-start(f32[3,2,144,128]{3,2,1,0:T(8,128)} %constant.26.clone.mask_ref) | copy-start | bytes 1327108
  0.0 2.3 %copy-start.3 = (s32[2,144,128]{2,1,0:T(8,128)S(1)}, s32[2,144,128]{2,1,0:T(8,128)}, u32[]{:S(2)}) copy-start(s32[2,144,128]{2,1,0:T(8,128)} %constant.25.clone.index_ref) | copy-start | bytes 442372
  0.0 2.3 %copy-start.8 = (bf16[128,128]{1,0:T(8,128)(2,1)S(1)}, bf16[128,128]{1,0:T(8,128)(2,1)}, u32[]{:S(2)}) copy-start(bf16[128,128]{1,0:T(8,128)(2,1)} %constant.24.clone.fold_ref) | copy-start | bytes 98308
  0.0 2.3 %copy-start.5 = (f32[256,128]{1,0:T(8,128)S(1)}, f32[256,128]{1,0:T(8,128)}, u32[]{:S(2)}) copy-start(f32[256,128]{1,0:T(8,128)} %constant.23.clone.rest_ref) | copy-start | bytes 393220
  0.0 2.3 %copy-start.9 = (bf16[16,256]{1,0:T(8,128)(2,1)S(1)}, bf16[16,256]{1,0:T(8,128)(2,1)}, u32[]{:S(2)}) copy-start(bf16[16,256]{1,0:T(8,128)(2,1)} %constant.22.clone.head_ref) | copy-start | bytes 24580
  0.0 2.3 %copy-start.6 = (bf16[256,256]{1,0:T(8,128)(2,1)S(1)}, bf16[256,256]{1,0:T(8,128)(2,1)}, u32[]{:S(2)}) copy-start(bf16[256,256]{1,0:T(8,128)(2,1)} %constant.21.clone.eye_ref) | copy-start | bytes 393220
  0.0 2.3 %copy-start.2 = (bf16[2,160,256]{2,1,0:T(8,128)(2,1)S(1)}, bf16[2,160,256]{2,1,0:T(8,128)(2,1)}, u32[]{:S(2)}) copy-start(bf16[2,160,256]{2,1,0:T(8,128)(2,1)} %constant.20.clone.perm_out_ref) | copy-start | bytes 491524
  0.1 2.3 %copy-start.4 = (bf16[2,144,160]{2,1,0:T(8,128)(2,1)S(1)}, bf16[2,144,160]{2,1,0:T(8,128)(2,1)}, u32[]{:S(2)}) copy-start(bf16[2,144,160]{2,1,0:T(8,128)(2,1)} %constant.19.clone.perm_in_ref) | copy-start | bytes 276484
  0.1 2.3 %copy-start.7 = (f32[2,16,759]{2,1,0:T(8,128)S(1)}, f32[2,16,759]{2,1,0:T(8,128)}, u32[]{:S(2)}) copy-start(f32[2,16,759]{2,1,0:T(8,128)} %table_ref.1) | copy-start | bytes 291460
  0.1 2.3 %copy-start = (bf16[2,512,512]{2,1,0:T(8,128)(2,1)S(1)}, bf16[2,512,512]{2,1,0:T(8,128)(2,1)}, u32[]{:S(2)}) copy-start(bf16[2,512,512]{2,1,0:T(8,128)(2,1)} %out_ref.1) | copy-start | bytes 3145732
  0.1 2.3 %copy-start.10 = (f32[2,512]{1,0:T(2,128)S(1)}, f32[2,512]{1,0:T(2,128)}, u32[]{:S(2)}) copy-start(f32[2,512]{1,0:T(2,128)} %gain_ref.1) | copy-start | bytes 12292
where the time goes:
time: 44.9 us; the launch traced here: 44.7 us
  Pallas kernels  40.2 us (90%)
  local copies, waits for them, and re-layouts  4.27 us (10%)
    pallas_call x1, Pallas kernels, shards(): pl.pallas_call(functools.partial(kernel, lat_count, lon_count), out_shape...  40.2 us
    reshape x2, local copies, waits for them, and re-layouts, shards(): x = atmosphere.reshape(2, 2, 2, 3, 2, 6, D).transpose(0, 2, 4, 1, 3, 5, 6)  1.97 us
    reshape x1, local copies, waits for them, and re-layouts, shards(): return result.reshape(4, 6, 12, D)  1.32 us

commit v1 on v0

v1 whole, which is shorter than its diff:
```python
import functools
import math

import jax
import jax.numpy as jnp
import ml_dtypes
import numpy as np
from jax import lax
from jax.experimental import pallas as pl
from jax.experimental.pallas import tpu as pltpu
from jax.sharding import PartitionSpec as P

D = 512
HEADS = 16
HEAD_DIM = 32
WIN = 144
QUAD = 40
ROWS = 4 * QUAD
HALF = 18
ROW = 24
LANES = HEADS * ROW
OFFSETS = 11 * ROW
TABLE = 759
EPSILON = 1e-05
LOG2E = math.log2(math.e)
SCORE_SCALE = LOG2E * HEAD_DIM ** (-0.5)
EXCLUDED = -1e30
TW, TE, BW, BE = 0, 1, 2, 3
MESH = pl.DeviceIdType.MESH


def token_places(shifted):
    places = np.full(ROWS, -1)
    for lat in range(2):
        for lon in range(2):
            for lev in range(2):
                for r in range(3):
                    for c in range(6):
                        a, l, o = lat * 3 + r, lev, lon * 6 + c
                        if shifted:
                            a, l, o = (a + 3) % 6, 1 - l, (o + 6) % 12
                        row = (lat * 2 + lon) * QUAD + lev * HALF + r * 6 + c
                        places[row] = a * ROW + l * 12 + o
    return places


def constants():
    bf16 = ml_dtypes.bfloat16
    perm_in = np.zeros((2, WIN, ROWS), np.float32)
    for block in range(2):
        for row, token in enumerate(token_places(block == 1)):
            if token >= 0:
                perm_in[block, token, row] = 1
    perm_out = perm_in.transpose(0, 2, 1).copy()
    pick = np.zeros((OFFSETS, 512), np.float32)
    for offset in range(OFFSETS):
        da, level, col = offset // ROW, offset // 12 % 2, offset % 12
        pick[offset, level * 253 + da * 23 + col] = 1
    level = np.arange(ROW)[:, None] // 12
    levels = np.where(level == np.arange(LANES)[None, :] // 12 % 2, 0, EXCLUDED)
    return perm_in.astype(bf16), perm_out.astype(bf16), pick.astype(bf16), levels.astype(np.float32)


CONSTANTS = constants()


def nt_dot(a, b):
    return lax.dot_general(a, b, (((1,), (1,)), ((), ())), preferred_element_type=jnp.float32)


def tn_dot(a, b):
    return lax.dot_general(a, b, (((0,), (0,)), ((), ())), preferred_element_type=jnp.float32)


def dot(a, b):
    return jnp.dot(a, b, preferred_element_type=jnp.float32)


def offset_bias(table, padded, moved, pick):
    padded[...] = jnp.zeros(padded.shape, jnp.float32)
    padded[:, :TABLE] = table * LOG2E
    row = lax.broadcasted_iota(jnp.int32, (8, 768), 0)
    for head in range(HEADS):
        line = jnp.broadcast_to(padded[head : head + 1, :], (8, 768))

        def ahead(steps):
            return pltpu.roll(line, 768 - steps, 1, stride=1, stride_axis=0)

        strips = (
            ahead(253 + 11),
            jnp.where(row < 4, ahead(253 + 3), ahead(11 + 4)),
            ahead(11 - 4),
        )
        for n, strip in enumerate(strips):
            moved[head * ROW + 8 * n : head * ROW + 8 * n + 8, :] = strip[:, :512]
    whole = moved[...]
    high = whole.astype(jnp.bfloat16)
    rest = whole - high.astype(jnp.float32)
    middle = rest.astype(jnp.bfloat16)
    low = (rest - middle.astype(jnp.float32)).astype(jnp.bfloat16)
    return (nt_dot(pick, high) + nt_dot(pick, middle)) + nt_dot(pick, low)


def normalised(state, gain):
    center = state - jnp.mean(state, axis=-1, keepdims=True)
    spread = jnp.mean(center * center, axis=-1, keepdims=True)
    return (center * lax.rsqrt(spread + EPSILON) * gain).astype(jnp.bfloat16)


def project(states, gain, perm_in, qkv):
    normed = jnp.concatenate(
        [dot(perm_in, normalised(state, gain)).astype(jnp.bfloat16) for state in states], axis=0
    )
    return (
        dot(normed, qkv[:, :D]),
        dot(normed, qkv[:, D : 2 * D]).astype(jnp.bfloat16),
        dot(normed, qkv[:, 2 * D :]).astype(jnp.bfloat16),
    )


def strip_of(tile, n):
    strip = 16 * tile + n
    return strip // 3, strip % 3, strip // 3 // 4


def attend(w, queries, keys, values, bias_at, perm_out, out):
    keys = keys[w * WIN : w * WIN + WIN]
    values = values[w * WIN : w * WIN + WIN]
    head_lane = lax.broadcasted_iota(jnp.int32, (8, 128), 1) // HEAD_DIM
    zero = jnp.zeros((8, 128), jnp.float32)
    units = [(a, tile) for a in range(6) for tile in range(3)]

    scores = {}
    for a, tile in units:
        strips = []
        for n in range(16):
            head, part, lanes = strip_of(tile, n)
            first = w * WIN + a * ROW + 8 * part
            own = jnp.where(
                head_lane == head % 4, queries[first : first + 8, 128 * lanes : 128 * lanes + 128], 0.0
            )
            strips.append(jnp.concatenate([own, zero] if lanes == tile else [zero, own], axis=1))
        masked = jnp.concatenate(strips, axis=0).astype(jnp.bfloat16)
        scores[a, tile] = nt_dot(keys[:, 128 * tile : 128 * tile + 256], masked)

    chances = {}
    for a, tile in units:
        score = scores[a, tile] * SCORE_SCALE + bias_at(a, slice(128 * tile, 128 * tile + 128))
        exponents = jnp.exp2(score - jnp.max(score, axis=0, keepdims=True))
        chances[a, tile] = (exponents * (1.0 / jnp.sum(exponents, axis=0, keepdims=True))).astype(
            jnp.bfloat16
        )

    mixed = {}
    for a, tile in units:
        product = tn_dot(chances[a, tile], values[:, 128 * tile : 128 * tile + 256])
        for n in range(16):
            head, part, lanes = strip_of(tile, n)
            first = 128 * (lanes - tile)
            own = product[8 * n : 8 * n + 8, first : first + 128]
            place = (a, part, lanes)
            mixed[place] = (
                jnp.where(head_lane == head % 4, own, mixed[place]) if place in mixed else own
            )
    mixed = jnp.concatenate(
        [
            jnp.concatenate([mixed[a, part, lanes] for lanes in range(4)], axis=1)
            for a in range(6)
            for part in range(3)
        ],
        axis=0,
    ).astype(jnp.bfloat16)
    mixed = dot(perm_out, mixed).astype(jnp.bfloat16)
    return dot(mixed, out)


def quad_rows(value, quad, start, stop):
    return value[quad * QUAD + start : quad * QUAD + stop]


def kernel(
    lat_count,
    lon_count,
    x_ref,
    gain_ref,
    qkv_hbm,
    out_hbm,
    table_ref,
    perm_in_ref,
    perm_out_ref,
    pick_ref,
    levels_ref,
    result_ref,
    qkv_ref,
    out_ref,
    padded,
    moved,
    bias0,
    bias1,
    sends,
    frame,
    backs,
    home,
    weight_sem,
    send_sem,
    recv_sem,
    back_send_sem,
    back_recv_sem,
):
    i = lax.axis_index("lat")
    j = lax.axis_index("lon")
    east = lax.rem(j + 1, lon_count)
    west = lax.rem(j + lon_count - 1, lon_count)
    inner = lat_count - 1
    is_first = (inner - i) // inner
    is_last = i // inner
    up, down = i - 1 + is_first, i + 1 - is_last

    def fetched(block):
        return (
            pltpu.make_async_copy(qkv_hbm.at[block], qkv_ref.at[block], weight_sem.at[block]),
            pltpu.make_async_copy(out_hbm.at[block], out_ref.at[block], weight_sem.at[2 + block]),
        )

    for block in range(2):
        for copy in fetched(block):
            copy.start()

    barrier = pltpu.get_barrier_semaphore()

    def greet(lat, lon):
        pl.semaphore_signal(barrier, inc=1, device_id=(lat, lon), device_id_type=MESH)

    greet(i, west)
    greet(i, east)

    @pl.when(i > 0)
    def _():
        greet(i - 1, j)
        greet(i - 1, west)

    @pl.when(i < inner)
    def _():
        greet(i + 1, j)
        greet(i + 1, east)

    bias0[...] = offset_bias(table_ref[0], padded, moved, pick_ref[...])

    def remote(src, dst, from_, to, lat, lon, rows, send, recv):
        which, quad = from_
        to_which, to_quad = to
        return pltpu.make_async_remote_copy(
            src_ref=src.at[which, quad, rows],
            dst_ref=dst.at[to_which, to_quad, rows],
            send_sem=send.at[which * 4 + quad],
            recv_sem=recv.at[to_which * 4 + to_quad],
            device_id=(lat, lon),
            device_id_type=MESH,
        )

    PIECES = ((slice(24, 40), slice(0, 16)), (slice(0, 24), slice(16, 40)))

    def outward(piece, which, quad, to_which, to_quad, lat, lon):
        return remote(
            sends,
            frame,
            (which, quad),
            (to_which, to_quad),
            lat,
            lon,
            PIECES[piece][which],
            send_sem.at[piece],
            recv_sem.at[piece],
        )

    def always_out(piece):
        return [
            outward(piece, 0, TW, is_first, TW + is_first * (BW - TW), up, west),
            outward(piece, 1, BE, 1 - is_last, BE - is_last * (BE - TE), down, east),
            outward(piece, 0, BW, 0, BW, i, west),
            outward(piece, 1, TE, 1, TE, i, east),
        ]

    def up_out(piece):
        return outward(piece, 0, TE, 0, TE, i - 1, j)

    def down_out(piece):
        return outward(piece, 1, BW, 1, BW, i + 1, j)

    def send(piece):
        for copy in always_out(piece):
            copy.start()

        @pl.when(i > 0)
        def _():
            up_out(piece).start()

        @pl.when(i < inner)
        def _():
            down_out(piece).start()

    def keep(which, quad, rows, value):
        stays = quad == (BE if which == 0 else TW)
        (frame if stays else sends)[which, quad, rows, :] = value

    for copy in fetched(0):
        copy.wait()
    packed = project([x_ref[0], x_ref[1]], gain_ref[0:1, :], perm_in_ref[0], qkv_ref[0])

    def plain_window(w):
        def bias_at(a, lanes):
            return bias0[(5 - a) * ROW : (5 - a) * ROW + WIN, lanes]

        return x_ref[w] + attend(w, *packed, bias_at, perm_out_ref[0], out_ref[0])

    lower = plain_window(0)
    for quad in range(4):
        keep(0, quad, slice(24, 40), quad_rows(lower, quad, 24, 40))
        keep(1, quad, slice(0, 16), quad_rows(lower, quad, 0, 16))
    pl.semaphore_wait(barrier, 2 + 2 * (1 - is_first) + 2 * (1 - is_last))
    send(0)

    upper = plain_window(1)
    short = lax.broadcasted_iota(jnp.int32, (8, D), 0) < HALF - 16
    for quad in range(4):
        low, high = quad_rows(lower, quad, 16, 24), quad_rows(upper, quad, 16, 24)
        keep(0, quad, slice(0, 16), quad_rows(upper, quad, 0, 16))
        keep(0, quad, slice(16, 24), jnp.where(short, high, low))
        keep(1, quad, slice(16, 24), jnp.where(short, low, high))
        keep(1, quad, slice(24, 40), quad_rows(upper, quad, 24, 40))
    send(1)

    @pl.when(i == 0)
    def _():
        frame[1, BE] = sends[0, TE]

    @pl.when(i == inner)
    def _():
        frame[0, TW] = sends[1, BW]

    last = is_last.astype(jnp.float32)
    first = is_first.astype(jnp.float32)
    bias0[...] = offset_bias(table_ref[1], padded, moved, pick_ref[...])
    for strip in range(11):
        rows = slice(strip * ROW, strip * ROW + ROW)
        levels = levels_ref[...]
        base = bias0[rows, :]
        split = base + levels
        bias1[0, 0, rows, :] = base + last * EXCLUDED
        bias1[0, 1, rows, :] = base + last * levels
        bias1[0, 2, rows, :] = base
        bias1[1, 0, rows, :] = split + first * EXCLUDED
        bias1[1, 1, rows, :] = split
        bias1[1, 2, rows, :] = base + (1 - first) * levels

    def arrived(ref, rows, sem, which, quad):
        here = ref.at[which, quad, rows]
        pltpu.make_async_copy(here, here, sem.at[which * 4 + quad]).wait()

    def came(which, quad):
        for piece in range(2):
            arrived(frame, PIECES[piece][which], recv_sem.at[piece], which, quad)

    for which, quad in ((0, BW), (0, TE), (1, TE), (1, BW)):
        came(which, quad)

    @pl.when(i < inner)
    def _():
        came(0, TW)

    @pl.when(i > 0)
    def _():
        came(1, BE)

    for copy in fetched(1):
        copy.wait()
    states = [frame[which].reshape(ROWS, D) for which in range(2)]
    packed1 = project(states, gain_ref[1:2, :], perm_in_ref[1], qkv_ref[1])

    def shifted_window(w):
        def bias_at(a, lanes):
            start = (5 - a) * ROW
            kinds = (2, 0) if a < 3 else (0, 1)
            return jnp.concatenate(
                [
                    bias1[w, kind, start + 72 * half : start + 72 * half + 72, lanes]
                    for half, kind in enumerate(kinds)
                ],
                axis=0,
            )

        result = states[w] + attend(w, *packed1, bias_at, perm_out_ref[1], out_ref[1])
        for quad in range(4):
            stays = quad == (BE if w == 0 else TW)
            (home if stays else backs)[w, quad] = quad_rows(result, quad, 0, QUAD)

    every = slice(0, QUAD)

    def backward(which, quad, to_which, to_quad, lat, lon):
        return remote(
            backs, home, (which, quad), (to_which, to_quad), lat, lon, every, back_send_sem, back_recv_sem
        )

    def first_back():
        return [
            backward(0, TE, is_last, TE + is_last * (BE - TE), down, j - is_last * (j - west)),
            backward(0, BW, 0, BW, i, east),
        ]

    def corner_back():
        return backward(0, TW, 0, TW, i + 1, east)

    shifted_window(0)
    for copy in first_back():
        copy.start()

    @pl.when(i < inner)
    def _():
        corner_back().start()

    @pl.when(i == inner)
    def _():
        home[1, BW] = backs[0, TW]

    def second_back():
        return [
            backward(1, BW, 1 - is_first, BW - is_first * (BW - TW), up, j - is_first * (j - east)),
            backward(1, TE, 1, TE, i, west),
        ]

    def other_corner_back():
        return backward(1, BE, 1, BE, i - 1, west)

    shifted_window(1)
    for copy in second_back():
        copy.start()

    @pl.when(i > 0)
    def _():
        other_corner_back().start()

    @pl.when(i == 0)
    def _():
        home[0, TE] = backs[1, BE]

    for which, quad in ((0, TW), (0, BW), (1, TE), (1, BE)):
        arrived(home, every, back_recv_sem, which, quad)

    @pl.when(i > 0)
    def _():
        arrived(home, every, back_recv_sem, 0, TE)

    @pl.when(i < inner)
    def _():
        arrived(home, every, back_recv_sem, 1, BW)

    ours = lax.broadcasted_iota(jnp.int32, (QUAD, D), 0) < HALF
    for quad in range(4):
        rows = slice(quad * QUAD, quad * QUAD + QUAD)
        mid, outer = home[0, quad], home[1, quad]
        result_ref[0, rows, :] = jnp.where(ours, outer, mid)
        result_ref[1, rows, :] = jnp.where(ours, mid, outer)

    for copy in always_out(0) + always_out(1) + first_back() + second_back():
        copy.wait_send()

    @pl.when(i > 0)
    def _():
        up_out(0).wait_send()
        up_out(1).wait_send()
        other_corner_back().wait_send()

    @pl.when(i < inner)
    def _():
        down_out(0).wait_send()
        down_out(1).wait_send()
        corner_back().wait_send()


def shards(lat_count, lon_count, atmosphere, norm_gain, qkv_weight, out_weight, position_bias):
    x = atmosphere.reshape(2, 2, 2, 3, 2, 6, D).transpose(0, 2, 4, 1, 3, 5, 6)
    x = x.reshape(2, 4, 2 * HALF, D)
    x = jnp.pad(x, ((0, 0), (0, 0), (0, QUAD - 2 * HALF), (0, 0))).reshape(2, ROWS, D)
    operands = [x, norm_gain, qkv_weight, out_weight, position_bias]
    operands += [jnp.asarray(c) for c in CONSTANTS]
    vmem, anywhere = pl.BlockSpec(memory_space=pltpu.VMEM), pl.BlockSpec(memory_space=pl.ANY)
    buffer = pltpu.VMEM((2, 4, QUAD, D), jnp.float32)
    result = pl.pallas_call(
        functools.partial(kernel, lat_count, lon_count),
        out_shape=jax.ShapeDtypeStruct((2, ROWS, D), jnp.float32),
        in_specs=[vmem, vmem, anywhere, anywhere] + [vmem] * (len(operands) - 4),
        out_specs=vmem,
        scratch_shapes=[
            pltpu.VMEM((2, D, 3 * D), jnp.bfloat16),
            pltpu.VMEM((2, D, D), jnp.bfloat16),
            pltpu.VMEM((HEADS, 768), jnp.float32),
            pltpu.VMEM((LANES, 512), jnp.float32),
            pltpu.VMEM((OFFSETS, LANES), jnp.float32),
            pltpu.VMEM((2, 3, OFFSETS, LANES), jnp.float32),
            buffer,
            buffer,
            buffer,
            buffer,
            pltpu.SemaphoreType.DMA((4,)),
            pltpu.SemaphoreType.DMA((2, 8)),
            pltpu.SemaphoreType.DMA((2, 8)),
            pltpu.SemaphoreType.DMA((8,)),
            pltpu.SemaphoreType.DMA((8,)),
        ],
        compiler_params=pltpu.CompilerParams(
            collective_id=0, has_side_effects=True, vmem_limit_bytes=48 * 1024 * 1024
        ),
    )(*operands)
    result = result.reshape(2, 4, QUAD, D)[:, :, : 2 * HALF]
    result = result.reshape(2, 2, 2, 2, 3, 6, D).transpose(0, 3, 1, 4, 2, 5, 6)
    return result.reshape(4, 6, 12, D)


def solution(mesh):
    in_specs = (P(None, "lat", "lon", None), P(), P(), P(), P())
    out_specs = P(None, "lat", "lon", None)
    body = functools.partial(shards, mesh.shape["lat"], mesh.shape["lon"])
    return jax.shard_map(body, mesh=mesh, in_specs=in_specs, out_specs=out_specs, check_vma=False)
```

time: 44.9 us -> 33.4 us (0.74)
  Pallas kernels: 40.2 us -> 26.7 us
  local copies, waits for them, and re-layouts: 4.27 us -> 6.23 us
    pallas_call x1, Pallas kernels: 40.2 us -> 26.7 us  [shards(): pl.pallas_call(functools.partial(kernel, lat_count, lon_count), out_shape...]
    reshape x2, local copies, waits for them, and re-layouts: 1.97 us -> 3.96 us  [shards(): x = atmosphere.reshape(2, 2, 2, 3, 2, 6, D).transpose(0, 2, 4, 1, 3, 5, 6)]
where the time goes in v1:
time: 33.4 us; the launch traced here: 33.1 us
  Pallas kernels  26.7 us (80%)
  local copies, waits for them, and re-layouts  6.23 us (19%)
    pallas_call x1, Pallas kernels, shards(): pl.pallas_call(functools.partial(kernel, lat_count, lon_count), out_shape...  26.7 us
    reshape x2, local copies, waits for them, and re-layouts, shards(): x = atmosphere.reshape(2, 2, 2, 3, 2, 6, D).transpose(0, 2, 4, 1, 3, 5, 6)  3.96 us
    reshape x1, local copies, waits for them, and re-layouts, shards(): return result.reshape(4, 6, 12, D)  1.32 us

profile of v1, /device:TPU:1, one launch (start us, length us, event | category | flops | bytes accessed | tf_op | source)
XLA Modules:
  0.0 33.1 jit_solution(5645370198539502311)
XLA Ops:
  0.0 0.0 copy-start.6
  0.0 0.0 copy-start.2
  0.0 0.0 copy-start.5
  0.0 0.0 copy-start
  0.0 0.0 copy-start.7
  0.0 2.5 %reshape.18 = f32[2,2,2,3,2,6,512]{6,1,0,5,4,3,2:T(2,128)} reshape(f32[4,6,12,512]{3,0,2,1:T(4,128)} %param.9) | data formatting | bytes 1179648 | tf_op jit(solution)/shard_map/reshape | solution.py:481
  2.5 0.0 copy-start.1
  2.5 0.0 copy-start.3
  2.5 0.0 copy-start.4
  2.5 1.5 %copy.15 = f32[2,2,2,3,2,6,512]{6,0,5,3,1,4,2:T(2,128)S(1)} copy(f32[2,2,2,3,2,6,512]{6,1,0,5,4,3,2:T(2,128)} %reshape.18) | data formatting | bytes 1179648 | tf_op jit(solution)/shard_map/reshape | solution.py:481
  4.0 0.1 copy.20
  4.2 0.0 copy-done.6
  4.2 0.0 copy-done.2
  4.2 0.0 copy-done.5
  4.2 0.0 copy-done
  4.2 0.0 copy-done.7
  4.2 0.0 copy-done.1
  4.2 0.0 copy-done.3
  4.2 0.0 copy-done.4
  4.3 26.7 %shard_map.91 = f32[2,160,512]{2,1,0:T(8,128)S(1)} custom-call(f32[2,160,512]{2,1,0:T(8,128)S(1)} %bitcast.13, f32[2,512]{1,0:T(2,128)S(1)} %copy-done.7, bf16[2,512,1536]{2,1,0:T(8,128)(2,1)S(1)} %copy-done, bf16[2,512,512]{2,1,0:T(8,128)(2,1)S(1)} %copy-done.1, f32[2,16,759]{2,1,0:T(8,128)S(1)} %copy-done.5, bf16[2,144,160]{2,1,0:T(8,128)(2,1)S(1)} %copy-done.4, ...), custom_call_target="tpu_custom_call" | custom-call | tf_op jit(solution)/shard_map/pallas_call | solution.py:488
  31.0 0.5 %copy.19 = f32[2,4,36,512]{3,0,2,1:T(2,128)S(1)} copy(f32[2,4,36,512]{3,2,1,0:T(8,128)S(1)} %bitcast.14) | data formatting | bytes 1179648
  31.5 0.3 copy.18
  31.8 1.3 %reshape.23 = f32[4,6,12,512]{3,0,2,1:T(4,128)} reshape(f32[2,2,2,3,2,6,512]{6,1,0,5,4,3,2:T(2,128)S(1)} %copy.18) | data formatting | bytes 1179648 | tf_op jit(solution)/shard_map/reshape | solution.py:516
  (1 shorter events, 0.0 us)
Async XLA Ops:
  0.0 4.2 %copy-start.6 = (f32[24,384]{1,0:T(8,128)S(1)}, f32[24,384]{1,0:T(8,128)}, u32[]{:S(2)}) copy-start(f32[24,384]{1,0:T(8,128)} %constant.14.clone.levels_ref) | copy-start | bytes 110596
  0.0 4.2 %copy-start.2 = (bf16[264,512]{1,0:T(8,128)(2,1)S(1)}, bf16[264,512]{1,0:T(8,128)(2,1)}, u32[]{:S(2)}) copy-start(bf16[264,512]{1,0:T(8,128)(2,1)} %constant.13.clone.pick_ref) | copy-start | bytes 811012
  0.0 4.2 %copy-start.5 = (f32[2,16,759]{2,1,0:T(8,128)S(1)}, f32[2,16,759]{2,1,0:T(8,128)}, u32[]{:S(2)}) copy-start(f32[2,16,759]{2,1,0:T(8,128)} %table_ref.1) | copy-start | bytes 291460
  0.0 4.2 %copy-start = (bf16[2,512,1536]{2,1,0:T(8,128)(2,1)S(1)}, bf16[2,512,1536]{2,1,0:T(8,128)(2,1)}, u32[]{:S(2)}) copy-start(bf16[2,512,1536]{2,1,0:T(8,128)(2,1)} %qkv_hbm.1) | copy-start | bytes 9437188
  0.0 4.2 %copy-start.7 = (f32[2,512]{1,0:T(2,128)S(1)}, f32[2,512]{1,0:T(2,128)}, u32[]{:S(2)}) copy-start(f32[2,512]{1,0:T(2,128)} %gain_ref.1) | copy-start | bytes 12292
  2.5 1.7 %copy-start.1 = (bf16[2,512,512]{2,1,0:T(8,128)(2,1)S(1)}, bf16[2,512,512]{2,1,0:T(8,128)(2,1)}, u32[]{:S(2)}) copy-start(bf16[2,512,512]{2,1,0:T(8,128)(2,1)} %out_hbm.1) | copy-start | bytes 3145732
  2.5 1.7 %copy-start.3 = (bf16[2,160,144]{2,1,0:T(8,128)(2,1)S(1)}, bf16[2,160,144]{2,1,0:T(8,128)(2,1)}, u32[]{:S(2)}) copy-start(bf16[2,160,144]{2,1,0:T(8,128)(2,1)} %constant.12.clone.perm_out_ref) | copy-start | bytes 276484
  2.5 1.7 %copy-start.4 = (bf16[2,144,160]{2,1,0:T(8,128)(2,1)S(1)}, bf16[2,144,160]{2,1,0:T(8,128)(2,1)}, u32[]{:S(2)}) copy-start(bf16[2,144,160]{2,1,0:T(8,128)(2,1)} %constant.11.clone.perm_in_ref) | copy-start | bytes 276484

commit v2 on v1

--- a/solution.py
+++ b/solution.py
@@ -174,6 +174,17 @@
     return dot(mixed, out)
 
 
+def strips():
+    for level in range(4):
+        for lat in range(2):
+            for lon in range(2):
+                for r in range(3):
+                    for tile in range(4):
+                        column = (lat * 3 + r) * 12 + lon * 6
+                        place = (lat * 2 + lon) * QUAD + level % 2 * HALF + r * 6
+                        yield (column * 4 + tile) * 4 + level, level // 2, place, tile
+
+
 def quad_rows(value, quad, start, stop):
     return value[quad * QUAD + start : quad * QUAD + stop]
 
@@ -181,7 +192,7 @@
 def kernel(
     lat_count,
     lon_count,
-    x_ref,
+    raw_hbm,
     gain_ref,
     qkv_hbm,
     out_hbm,
@@ -191,6 +202,8 @@
     pick_ref,
     levels_ref,
     result_ref,
+    raw_ref,
+    x_ref,
     qkv_ref,
     out_ref,
     padded,
@@ -222,6 +235,8 @@
             pltpu.make_async_copy(out_hbm.at[block], out_ref.at[block], weight_sem.at[2 + block]),
         )
 
+    raw_copy = pltpu.make_async_copy(raw_hbm, raw_ref, weight_sem.at[4])
+    raw_copy.start()
     for block in range(2):
         for copy in fetched(block):
             copy.start()
@@ -302,6 +317,16 @@
     def keep(which, quad, rows, value):
         stays = quad == (BE if which == 0 else TW)
         (frame if stays else sends)[which, quad, rows, :] = value
+
+    raw_copy.wait()
+    for quad in range(4):
+        end = quad * QUAD + QUAD
+        for w in range(2):
+            x_ref[w, end - 8 : end, :] = jnp.zeros((8, D), jnp.float32)
+    for first_row, w, place, tile in strips():
+        x_ref[w, place : place + 6, 128 * tile : 128 * tile + 128] = raw_ref[
+            pl.ds(first_row, 6, stride=16), :
+        ]
 
     for copy in fetched(0):
         copy.wait()
@@ -454,12 +479,12 @@
     def _():
         arrived(home, every, back_recv_sem, 1, BW)
 
-    ours = lax.broadcasted_iota(jnp.int32, (QUAD, D), 0) < HALF
-    for quad in range(4):
-        rows = slice(quad * QUAD, quad * QUAD + QUAD)
-        mid, outer = home[0, quad], home[1, quad]
-        result_ref[0, rows, :] = jnp.where(ours, outer, mid)
-        result_ref[1, rows, :] = jnp.where(ours, mid, outer)
+    for first_row, w, place, tile in strips():
+        quad, row = place // QUAD, place % QUAD
+        which = 1 if (w == 0) == (row < HALF) else 0
+        result_ref[pl.ds(first_row, 6, stride=16), :] = home[
+            which, quad, row : row + 6, 128 * tile : 128 * tile + 128
+        ]
 
     for copy in always_out(0) + always_out(1) + first_back() + second_back():
         copy.wait_send()
@@ -478,19 +503,20 @@
 
 
 def shards(lat_count, lon_count, atmosphere, norm_gain, qkv_weight, out_weight, position_bias):
-    x = atmosphere.reshape(2, 2, 2, 3, 2, 6, D).transpose(0, 2, 4, 1, 3, 5, 6)
-    x = x.reshape(2, 4, 2 * HALF, D)
-    x = jnp.pad(x, ((0, 0), (0, 0), (0, QUAD - 2 * HALF), (0, 0))).reshape(2, ROWS, D)
+    x = atmosphere.transpose(1, 2, 0, 3).reshape(6, 12, 4, 4, 128)
+    x = x.transpose(0, 1, 3, 2, 4).reshape(1152, 128)
     operands = [x, norm_gain, qkv_weight, out_weight, position_bias]
     operands += [jnp.asarray(c) for c in CONSTANTS]
     vmem, anywhere = pl.BlockSpec(memory_space=pltpu.VMEM), pl.BlockSpec(memory_space=pl.ANY)
     buffer = pltpu.VMEM((2, 4, QUAD, D), jnp.float32)
     result = pl.pallas_call(
         functools.partial(kernel, lat_count, lon_count),
-        out_shape=jax.ShapeDtypeStruct((2, ROWS, D), jnp.float32),
-        in_specs=[vmem, vmem, anywhere, anywhere] + [vmem] * (len(operands) - 4),
+        out_shape=jax.ShapeDtypeStruct((1152, 128), jnp.float32),
+        in_specs=[anywhere, vmem, anywhere, anywhere] + [vmem] * (len(operands) - 4),
         out_specs=vmem,
         scratch_shapes=[
+            pltpu.VMEM((1152, 128), jnp.float32),
+            pltpu.VMEM((2, ROWS, D), jnp.float32),
             pltpu.VMEM((2, D, 3 * D), jnp.bfloat16),
             pltpu.VMEM((2, D, D), jnp.bfloat16),
             pltpu.VMEM((HEADS, 768), jnp.float32),
@@ -501,19 +527,18 @@
             buffer,
             buffer,
             buffer,
-            pltpu.SemaphoreType.DMA((4,)),
+            pltpu.SemaphoreType.DMA((5,)),
             pltpu.SemaphoreType.DMA((2, 8)),
             pltpu.SemaphoreType.DMA((2, 8)),
             pltpu.SemaphoreType.DMA((8,)),
             pltpu.SemaphoreType.DMA((8,)),
         ],
         compiler_params=pltpu.CompilerParams(
-            collective_id=0, has_side_effects=True, vmem_limit_bytes=48 * 1024 * 1024
+            collective_id=0, has_side_effects=True, vmem_limit_bytes=60 * 1024 * 1024
         ),
     )(*operands)
-    result = result.reshape(2, 4, QUAD, D)[:, :, : 2 * HALF]
-    result = result.reshape(2, 2, 2, 2, 3, 6, D).transpose(0, 3, 1, 4, 2, 5, 6)
-    return result.reshape(4, 6, 12, D)
+    result = result.reshape(6, 12, 4, 4, 128).transpose(0, 1, 3, 2, 4)
+    return result.reshape(6, 12, 4, D).transpose(2, 0, 1, 3)
 
 
 def solution(mesh):

time: 33.4 us -> 30.8 us (0.922)
  local copies, waits for them, and re-layouts: 6.23 us -> 1.94 us
  Pallas kernels: 26.7 us -> 28.5 us
    reshape x3 -> x0, local copies, waits for them, and re-layouts: 5.28 us -> none  [the longest x2 3.96 us: shards(): x = atmosphere.reshape(2, 2, 2, 3, 2, 6, D).transpose(0, 2, 4, 1, 3, 5, 6)]
    pallas_call x1, Pallas kernels: 26.7 us -> 28.5 us  [shards(): pl.pallas_call(functools.partial(kernel, lat_count, lon_count), out_shape...]
    unnamed x18 -> x1, local copies, waits for them, and re-layouts: 0.6 us -> 1.94 us
where the time goes in v2:
time: 30.8 us; the launch traced here: 30.5 us
  Pallas kernels  28.5 us (93%)
  local copies, waits for them, and re-layouts  1.94 us (6%)
    pallas_call x1, Pallas kernels, shards(): pl.pallas_call(functools.partial(kernel, lat_count, lon_count), out_shape...  28.5 us
    unnamed x1, local copies, waits for them, and re-layouts  1.94 us

profile of v2, /device:TPU:1, one launch (start us, length us, event | category | flops | bytes accessed | tf_op | source)
XLA Modules:
  0.0 30.5 jit_solution(18054833737189625301)
XLA Ops:
  0.0 28.5 %shard_map.91 = f32[1152,128]{1,0:T(8,128)} custom-call(f32[1152,128]{1,0:T(8,128)} %bitcast.15, f32[2,512]{1,0:T(2,128)} %gain_ref.1, bf16[2,512,1536]{2,1,0:T(8,128)(2,1)} %qkv_hbm.1, bf16[2,512,512]{2,1,0:T(8,128)(2,1)} %out_hbm.1, f32[2,16,759]{2,1,0:T(8,128)} %table_ref.1, bf16[2,144,160]{2,1,0:T(8,128)(2,1)} %constant.8.clone.perm_in_ref, ...), custom_call_target="tpu_custom_call" | custom-call | tf_op jit(solution)/shard_map/pallas_call | solution.py:512
  28.6 1.9 %copy.12 = f32[4,6,12,512]{3,0,2,1:T(4,128)} copy(f32[4,6,12,512]{3,0,2,1:T(4,128)} %bitcast.14) | data formatting | bytes 1179648

commit v3 on v2

v3 whole, which is shorter than its diff:
```python
import functools
import math

import jax
import jax.numpy as jnp
import ml_dtypes
import numpy as np
from jax import lax
from jax.experimental import pallas as pl
from jax.experimental.pallas import tpu as pltpu
from jax.sharding import PartitionSpec as P

D = 512
HEADS = 16
HEAD_DIM = 32
WIN = 144
QUAD = 40
ROWS = 4 * QUAD
HALF = 18
ROW = 24
LANES = HEADS * ROW
OFFSETS = 11 * ROW
PAIRED = 10 * ROW
TABLE = 759
EPSILON = 1e-05
LOG2E = math.log2(math.e)
SCORE_SCALE = LOG2E * HEAD_DIM ** (-0.5)
EXCLUDED = -1e30
TW, TE, BW, BE = 0, 1, 2, 3
MESH = pl.DeviceIdType.MESH


def token_places(shifted):
    places = np.full(ROWS, -1)
    for lat in range(2):
        for lon in range(2):
            for lev in range(2):
                for r in range(3):
                    for c in range(6):
                        a, l, o = lat * 3 + r, lev, lon * 6 + c
                        if shifted:
                            a, l, o = (a + 3) % 6, 1 - l, (o + 6) % 12
                        row = (lat * 2 + lon) * QUAD + lev * HALF + r * 6 + c
                        places[row] = a * ROW + l * 12 + o
    return places


def constants():
    bf16 = ml_dtypes.bfloat16
    plain, shifted = token_places(False), token_places(True)

    def one_hot(count, tokens):
        return (np.arange(count)[:, None] == tokens[None, :]).astype(bf16)

    perm_in = np.stack([one_hot(WIN, plain), one_hot(WIN, shifted)])
    col = shifted % 12
    eastern = (shifted >= 0) & (col < 6)
    western = (shifted >= 0) & (col >= 6)
    own = np.where(eastern, shifted // 12 * 6 + col, np.where(western, 72 + shifted // 12 * 6 + col - 6, -1))
    perm_query = np.concatenate(
        [one_hot(WIN, np.where(eastern, own, -1)), one_hot(WIN, np.where(western, own, -1))], axis=1
    )
    perm_out = np.stack([one_hot(WIN, plain).T, one_hot(WIN, own).T])
    offset = np.arange(OFFSETS)
    index = offset // 12 % 2 * 253 + offset // ROW * 23 + offset % 12
    pick0 = (index[:, None] == np.arange(512)[None, :]).astype(bf16)
    index = np.concatenate([index[:PAIRED] + 13, index[:PAIRED] + 7])
    pick1 = (index[:, None] == np.arange(512)[None, :]).astype(bf16)
    lane = np.arange(LANES)[None, :]
    levels = np.where(np.arange(ROW)[:, None] // 12 == lane // 6 % 2, 0, EXCLUDED)
    second = np.broadcast_to(lane // 12 % 2, (ROW, LANES))
    marks = np.stack([levels, second]).astype(np.float32)
    return perm_in, perm_query, perm_out, pick0, pick1, marks


CONSTANTS = constants()


def nt_dot(a, b):
    return lax.dot_general(a, b, (((1,), (1,)), ((), ())), preferred_element_type=jnp.float32)


def tn_dot(a, b):
    return lax.dot_general(a, b, (((0,), (0,)), ((), ())), preferred_element_type=jnp.float32)


def dot(a, b):
    return jnp.dot(a, b, preferred_element_type=jnp.float32)


def offset_bias(table, padded, moved, pick, paired):
    padded[...] = jnp.zeros(padded.shape, jnp.float32)
    padded[:, :TABLE] = table * LOG2E
    row = lax.broadcasted_iota(jnp.int32, (8, 768), 0)
    for head in range(HEADS):
        line = jnp.broadcast_to(padded[head : head + 1, :], (8, 768))

        def ahead(steps):
            return pltpu.roll(line, (768 - steps) % 768, 1, stride=1, stride_axis=0)

        if paired:
            strips = (
                jnp.where(row < 6, ahead(274), ahead(27)),
                jnp.where(row < 4, ahead(19), ahead(255)),
                jnp.where(row < 2, ahead(247), ahead(0)),
            )
        else:
            strips = (
                ahead(253 + 11),
                jnp.where(row < 4, ahead(253 + 3), ahead(11 + 4)),
                ahead(11 - 4),
            )
        for n, strip in enumerate(strips):
            moved[head * ROW + 8 * n : head * ROW + 8 * n + 8, :] = strip[:, :512]
    whole = moved[...]
    high = whole.astype(jnp.bfloat16)
    rest = whole - high.astype(jnp.float32)
    middle = rest.astype(jnp.bfloat16)
    low = (rest - middle.astype(jnp.float32)).astype(jnp.bfloat16)
    return (nt_dot(pick, high) + nt_dot(pick, middle)) + nt_dot(pick, low)


def normalised(state, gain):
    center = state - jnp.mean(state, axis=-1, keepdims=True)
    spread = jnp.mean(center * center, axis=-1, keepdims=True)
    return (center * lax.rsqrt(spread + EPSILON) * gain).astype(jnp.bfloat16)


def rounded(value):
    return value.astype(jnp.bfloat16)


def strip_of(tile, n):
    strip = 16 * tile + n
    return strip // 3, strip % 3, strip // 3 // 4


def attend(queries, windows, bias_at):
    head_lane = lax.broadcasted_iota(jnp.int32, (8, 128), 1) // HEAD_DIM
    zero = jnp.zeros((8, 128), jnp.float32)
    units = [
        (which, a, tile) for which, window in enumerate(windows) for a in window[2] for tile in range(3)
    ]

    scores = {}
    for which, a, tile in units:
        strips = []
        for n in range(16):
            head, part, lanes = strip_of(tile, n)
            first = a * ROW + 8 * part
            own = jnp.where(
                head_lane == head % 4, queries[first : first + 8, 128 * lanes : 128 * lanes + 128], 0.0
            )
            strips.append(jnp.concatenate([own, zero] if lanes == tile else [zero, own], axis=1))
        masked = rounded(jnp.concatenate(strips, axis=0))
        scores[a, tile] = nt_dot(windows[which][0][:, 128 * tile : 128 * tile + 256], masked)

    chances = {}
    for which, a, tile in units:
        score = scores[a, tile] * SCORE_SCALE + bias_at(a, slice(128 * tile, 128 * tile + 128))
        exponents = jnp.exp2(score - jnp.max(score, axis=0, keepdims=True))
        chances[a, tile] = rounded(exponents * (1.0 / jnp.sum(exponents, axis=0, keepdims=True)))

    mixed = {}
    for which, a, tile in units:
        product = tn_dot(chances[a, tile], windows[which][1][:, 128 * tile : 128 * tile + 256])
        for n in range(16):
            head, part, lanes = strip_of(tile, n)
            first = 128 * (lanes - tile)
            own = product[8 * n : 8 * n + 8, first : first + 128]
            place = (a, part, lanes)
            mixed[place] = (
                jnp.where(head_lane == head % 4, own, mixed[place]) if place in mixed else own
            )
    rows = [a for window in windows for a in window[2]]
    return jnp.concatenate(
        [
            jnp.concatenate([mixed[a, part, lanes] for lanes in range(4)], axis=1)
            for a in rows
            for part in range(3)
        ],
        axis=0,
    )


def projected(mixed, perm_out, out):
    mixed = rounded(dot(perm_out, rounded(mixed)))
    return dot(mixed, out)


def strips():
    for level in range(4):
        for lat in range(2):
            for lon in range(2):
                for r in range(3):
                    for tile in range(4):
                        column = (lat * 3 + r) * 12 + lon * 6
                        place = (lat * 2 + lon) * QUAD + level % 2 * HALF + r * 6
                        yield (column * 4 + tile) * 4 + level, level // 2, place, tile


def quad_rows(value, quad, start, stop):
    return value[quad * QUAD + start : quad * QUAD + stop]


def kernel(
    lat_count,
    lon_count,
    raw_hbm,
    gain_ref,
    qkv_hbm,
    out_hbm,
    table_ref,
    perm_in_ref,
    perm_query_ref,
    perm_out_ref,
    pick0_ref,
    pick1_ref,
    marks_ref,
    result_ref,
    raw_ref,
    x_ref,
    qkv_ref,
    out_ref,
    padded,
    moved,
    bias0,
    offsets1,
    bias1,
    mine,
    frame,
    backs,
    home,
    weight_sem,
    send_sem,
    recv_sem,
    back_send_sem,
    back_recv_sem,
):
    i = lax.axis_index("lat")
    j = lax.axis_index("lon")
    east = lax.rem(j + 1, lon_count)
    west = lax.rem(j + lon_count - 1, lon_count)
    inner = lat_count - 1
    is_first = (inner - i) // inner
    is_last = i // inner
    up, down = i - 1 + is_first, i + 1 - is_last

    def fetched(block):
        return (
            pltpu.make_async_copy(qkv_hbm.at[block], qkv_ref.at[block], weight_sem.at[block]),
            pltpu.make_async_copy(out_hbm.at[block], out_ref.at[block], weight_sem.at[2 + block]),
        )

    raw_copy = pltpu.make_async_copy(raw_hbm, raw_ref, weight_sem.at[4])
    raw_copy.start()
    for block in range(2):
        for copy in fetched(block):
            copy.start()

    barrier = pltpu.get_barrier_semaphore()

    def greet(lat, lon):
        pl.semaphore_signal(barrier, inc=1, device_id=(lat, lon), device_id_type=MESH)

    greet(i, west)
    greet(i, east)

    @pl.when(i > 0)
    def _():
        for lon in (west, j, east):
            greet(i - 1, lon)

    @pl.when(i < inner)
    def _():
        for lon in (west, j, east):
            greet(i + 1, lon)

    bias0[...] = offset_bias(table_ref[0], padded, moved, pick0_ref[...], False)

    PIECES = ((slice(24, 40), slice(0, 16)), (slice(0, 24), slice(16, 40)))
    E, W = 0, 1

    def outward(piece, number, which, quad, to, lat, lon):
        rows = PIECES[piece][which]
        return pltpu.make_async_remote_copy(
            src_ref=mine.at[which, quad, rows],
            dst_ref=frame.at[to[0], to[1], to[2], rows],
            send_sem=send_sem.at[piece, number],
            recv_sem=recv_sem.at[piece, to[0] * 8 + to[1] * 4 + to[2]],
            device_id=(lat, lon),
            device_id_type=MESH,
        )

    def always_out(piece):
        top, bottom = is_first * (BW - TW), is_last * (BW - TW)
        return [
            outward(piece, 0, 0, TE, (is_first, W, TE + top), up, east),
            outward(piece, 1, 0, TW, (is_first, E, TW + top), up, west),
            outward(piece, 2, 1, BE, (1 - is_last, W, BE - bottom), down, east),
            outward(piece, 3, 1, BW, (1 - is_last, E, BW - bottom), down, west),
            outward(piece, 4, 0, BE, (0, W, BE), i, east),
            outward(piece, 5, 0, BW, (0, E, BW), i, west),
            outward(piece, 6, 1, TE, (1, W, TE), i, east),
            outward(piece, 7, 1, TW, (1, E, TW), i, west),
        ]

    def up_out(piece):
        return [
            outward(piece, 8, 0, TE, (0, E, TE), i - 1, j),
            outward(piece, 9, 0, TW, (0, W, TW), i - 1, j),
        ]

    def down_out(piece):
        return [
            outward(piece, 10, 1, BE, (1, E, BE), i + 1, j),
            outward(piece, 11, 1, BW, (1, W, BW), i + 1, j),
        ]

    def send(piece):
        for copy in always_out(piece):
            copy.start()

        @pl.when(i > 0)
        def _():
            for copy in up_out(piece):
                copy.start()

        @pl.when(i < inner)
        def _():
            for copy in down_out(piece):
                copy.start()

    def keep(which, quad, rows, value):
        mine[which, quad, rows, :] = value
        if quad in ((BW, BE), (TW, TE))[which]:
            frame[which, E if quad in (TE, BE) else W, quad, rows, :] = value

    raw_copy.wait()
    for quad in range(4):
        end = quad * QUAD + QUAD
        for w in range(2):
            x_ref[w, end - 8 : end, :] = jnp.zeros((8, D), jnp.float32)
    for first_row, w, place, tile in strips():
        x_ref[w, place : place + 6, 128 * tile : 128 * tile + 128] = raw_ref[
            pl.ds(first_row, 6, stride=16), :
        ]

    for copy in fetched(0):
        copy.wait()
    qkv = qkv_ref[0]
    normed = jnp.concatenate(
        [rounded(dot(perm_in_ref[0], normalised(x_ref[w], gain_ref[0:1, :]))) for w in range(2)], axis=0
    )
    queries0 = dot(normed, qkv[:, :D])
    keys0 = rounded(dot(normed, qkv[:, D : 2 * D]))
    values0 = rounded(dot(normed, qkv[:, 2 * D :]))

    def plain_window(w):
        def bias_at(a, lanes):
            start = (5 - (a - 6 * w)) * ROW
            return bias0[start : start + WIN, lanes]

        rows = slice(w * WIN, w * WIN + WIN)
        window = (keys0[rows], values0[rows], range(6 * w, 6 * w + 6))
        mixed = attend(queries0, [window], bias_at)
        return x_ref[w] + projected(mixed, perm_out_ref[0], out_ref[0])

    lower = plain_window(0)
    for quad in range(4):
        keep(0, quad, slice(24, 40), quad_rows(lower, quad, 24, 40))
        keep(1, quad, slice(0, 16), quad_rows(lower, quad, 0, 16))
    pl.semaphore_wait(barrier, 2 + 3 * (1 - is_first) + 3 * (1 - is_last))
    send(0)

    upper = plain_window(1)
    short = lax.broadcasted_iota(jnp.int32, (8, D), 0) < HALF - 16
    for quad in range(4):
        low, high = quad_rows(lower, quad, 16, 24), quad_rows(upper, quad, 16, 24)
        keep(0, quad, slice(0, 16), quad_rows(upper, quad, 0, 16))
        keep(0, quad, slice(16, 24), jnp.where(short, high, low))
        keep(1, quad, slice(16, 24), jnp.where(short, low, high))
        keep(1, quad, slice(24, 40), quad_rows(upper, quad, 24, 40))
    send(1)

    @pl.when(i == 0)
    def _():
        frame[1, E, BE] = mine[0, TE]
        frame[1, W, BW] = mine[0, TW]

    @pl.when(i == inner)
    def _():
        frame[0, E, TE] = mine[1, BE]
        frame[0, W, TW] = mine[1, BW]

    last = is_last.astype(jnp.float32)
    first = is_first.astype(jnp.float32)
    offsets1[...] = offset_bias(table_ref[1], padded, moved, pick1_ref[...], True)
    levels, in_second = marks_ref[0], marks_ref[1] > 0.5
    same = ((jnp.zeros((ROW, LANES), jnp.float32), last * levels), ((1 - first) * levels, levels))
    cross = (jnp.full((ROW, LANES), last * EXCLUDED), levels + first * EXCLUDED)
    for which in range(2):
        bottom, top = same[which]
        apart = cross[which]
        added = (
            (bottom, apart),
            (jnp.where(in_second, apart, bottom), jnp.where(in_second, top, apart)),
            (apart, top),
        )
        for win in range(2):
            for pair in range(3):
                start = win * PAIRED + (4 - 2 * pair) * ROW
                for strip in range(6):
                    rows = slice(start + strip * ROW, start + strip * ROW + ROW)
                    bias1[which, win * 3 + pair, strip * ROW : strip * ROW + ROW, :] = (
                        offsets1[rows, :] + added[pair][strip // 3]
                    )

    def arrived(which, win, quad):
        for piece in range(2):
            here = frame.at[which, win, quad, PIECES[piece][which]]
            sem = recv_sem.at[piece, which * 8 + win * 4 + quad]
            pltpu.make_async_copy(here, here, sem).wait()

    for which in range(2):
        for win, quad in ((E, TW), (E, BW), (W, TE), (W, BE)):
            arrived(which, win, quad)

    @pl.when(i < inner)
    def _():
        arrived(0, E, TE)
        arrived(0, W, TW)

    @pl.when(i > 0)
    def _():
        arrived(1, E, BE)
        arrived(1, W, BW)

    for copy in fetched(1):
        copy.wait()
    qkv = qkv_ref[1]
    normed = [
        normalised(frame[which, win].reshape(ROWS, D), gain_ref[1:2, :])
        for which in range(2)
        for win in range(2)
    ]
    asking = jnp.concatenate(
        [
            rounded(dot(perm_query_ref[...], jnp.concatenate(normed[2 * which : 2 * which + 2], axis=0)))
            for which in range(2)
        ],
        axis=0,
    )
    queries1 = dot(asking, qkv[:, :D])
    normed = jnp.concatenate([rounded(dot(perm_in_ref[1], n)) for n in normed], axis=0)
    keys1 = rounded(dot(normed, qkv[:, D : 2 * D]))
    values1 = rounded(dot(normed, qkv[:, 2 * D :]))

    def shifted_rows(which):
        def bias_at(a, lanes):
            return bias1[which, a - 6 * which, :, lanes]

        windows = []
        for win in range(2):
            rows = slice((2 * which + win) * WIN, (2 * which + win) * WIN + WIN)
            start = 6 * which + 3 * win
            windows.append((keys1[rows], values1[rows], range(start, start + 3)))
        mixed = attend(queries1, windows, bias_at)
        result = projected(mixed, perm_out_ref[1], out_ref[1])
        stay = ((BW, BE), (TW, TE))[which]
        for quad in range(4):
            state = frame[which, E if quad in (TE, BE) else W, quad]
            value = state + quad_rows(result, quad, 0, QUAD)
            if quad in stay:
                home[which, quad] = value
            else:
                backs[which, quad % 2] = value

    def backward(which, lat):
        place = slice(0, 2) if which == 0 else slice(2, 4)
        return pltpu.make_async_remote_copy(
            src_ref=backs.at[which],
            dst_ref=home.at[which, place],
            send_sem=back_send_sem.at[which],
            recv_sem=back_recv_sem.at[which],
            device_id=(lat, j),
            device_id_type=MESH,
        )

    shifted_rows(0)

    @pl.when(i < inner)
    def _():
        backward(0, i + 1).start()

    @pl.when(i == inner)
    def _():
        home[1, 2:4] = backs[0]

    shifted_rows(1)

    @pl.when(i > 0)
    def _():
        backward(1, i - 1).start()

    @pl.when(i == 0)
    def _():
        home[0, 0:2] = backs[1]

    @pl.when(i > 0)
    def _():
        backward(0, i - 1).wait_recv()

    @pl.when(i < inner)
    def _():
        backward(1, i + 1).wait_recv()

    for first_row, w, place, tile in strips():
        quad, row = place // QUAD, place % QUAD
        which = 1 if (w == 0) == (row < HALF) else 0
        result_ref[pl.ds(first_row, 6, stride=16), :] = home[
            which, quad, row : row + 6, 128 * tile : 128 * tile + 128
        ]

    for piece in range(2):
        for copy in always_out(piece):
            copy.wait_send()

    @pl.when(i > 0)
    def _():
        for copy in up_out(0) + up_out(1) + [backward(1, i - 1)]:
            copy.wait_send()

    @pl.when(i < inner)
    def _():
        for copy in down_out(0) + down_out(1) + [backward(0, i + 1)]:
            copy.wait_send()


def shards(lat_count, lon_count, atmosphere, norm_gain, qkv_weight, out_weight, position_bias):
    x = atmosphere.transpose(1, 2, 0, 3).reshape(6, 12, 4, 4, 128)
    x = x.transpose(0, 1, 3, 2, 4).reshape(1152, 128)
    operands = [x, norm_gain, qkv_weight, out_weight, position_bias]
    operands += [jnp.asarray(c) for c in CONSTANTS]
    vmem, anywhere = pl.BlockSpec(memory_space=pltpu.VMEM), pl.BlockSpec(memory_space=pl.ANY)
    result = pl.pallas_call(
        functools.partial(kernel, lat_count, lon_count),
        out_shape=jax.ShapeDtypeStruct((1152, 128), jnp.float32),
        in_specs=[anywhere, vmem, anywhere, anywhere] + [vmem] * (len(operands) - 4),
        out_specs=vmem,
        scratch_shapes=[
            pltpu.VMEM((1152, 128), jnp.float32),
            pltpu.VMEM((2, ROWS, D), jnp.float32),
            pltpu.VMEM((2, D, 3 * D), jnp.bfloat16),
            pltpu.VMEM((2, D, D), jnp.bfloat16),
            pltpu.VMEM((HEADS, 768), jnp.float32),
            pltpu.VMEM((LANES, 512), jnp.float32),
            pltpu.VMEM((OFFSETS, LANES), jnp.float32),
            pltpu.VMEM((2 * PAIRED, LANES), jnp.float32),
            pltpu.VMEM((2, 6, WIN, LANES), jnp.float32),
            pltpu.VMEM((2, 4, QUAD, D), jnp.float32),
            pltpu.VMEM((2, 2, 4, QUAD, D), jnp.float32),
            pltpu.VMEM((2, 2, QUAD, D), jnp.float32),
            pltpu.VMEM((2, 4, QUAD, D), jnp.float32),
            pltpu.SemaphoreType.DMA((5,)),
            pltpu.SemaphoreType.DMA((2, 12)),
            pltpu.SemaphoreType.DMA((2, 16)),
            pltpu.SemaphoreType.DMA((2,)),
            pltpu.SemaphoreType.DMA((2,)),
        ],
        compiler_params=pltpu.CompilerParams(
            collective_id=0, has_side_effects=True, vmem_limit_bytes=60 * 1024 * 1024
        ),
    )(*operands)
    result = result.reshape(6, 12, 4, 4, 128).transpose(0, 1, 3, 2, 4)
    return result.reshape(6, 12, 4, D).transpose(2, 0, 1, 3)


def solution(mesh):
    in_specs = (P(None, "lat", "lon", None), P(), P(), P(), P())
    out_specs = P(None, "lat", "lon", None)
    body = functools.partial(shards, mesh.shape["lat"], mesh.shape["lon"])
    return jax.shard_map(body, mesh=mesh, in_specs=in_specs, out_specs=out_specs, check_vma=False)
```

time: 30.8 us -> 34.7 us (1.13)
  Pallas kernels: 28.5 us -> 32.6 us
    pallas_call x1, Pallas kernels: 28.5 us -> 32.6 us  [shards(): pl.pallas_call(functools.partial(kernel, lat_count, lon_count), out_shape...]
where the time goes in v3:
time: 34.7 us; the launch traced here: 34.5 us
  Pallas kernels  32.6 us (94%)
  local copies, waits for them, and re-layouts  1.94 us (6%)
    pallas_call x1, Pallas kernels, shards(): pl.pallas_call(functools.partial(kernel, lat_count, lon_count), out_shape...  32.6 us
    unnamed x1, local copies, waits for them, and re-layouts  1.94 us

profile of v3, /device:TPU:1, one launch (start us, length us, event | category | flops | bytes accessed | tf_op | source)
XLA Modules:
  0.0 34.5 jit_solution(16510345539926950409)
XLA Ops:
  0.0 32.6 %shard_map.109 = f32[1152,128]{1,0:T(8,128)} custom-call(f32[1152,128]{1,0:T(8,128)} %bitcast.15, f32[2,512]{1,0:T(2,128)} %gain_ref.1, bf16[2,512,1536]{2,1,0:T(8,128)(2,1)} %qkv_hbm.1, bf16[2,512,512]{2,1,0:T(8,128)(2,1)} %out_hbm.1, f32[2,16,759]{2,1,0:T(8,128)} %table_ref.1, bf16[2,144,160]{2,1,0:T(8,128)(2,1)} %constant.12.clone.perm_in_ref, ...), custom_call_target="tpu_custom_call" | custom-call | tf_op jit(solution)/shard_map/pallas_call | solution.py:546
  32.6 1.9 %copy.14 = f32[4,6,12,512]{3,0,2,1:T(4,128)} copy(f32[4,6,12,512]{3,0,2,1:T(4,128)} %bitcast.14) | data formatting | bytes 1179648

commit v4 on v3

--- a/solution.py
+++ b/solution.py
@@ -207,9 +207,21 @@
     lat_count,
     lon_count,
     raw_hbm,
-    gain_ref,
+    gain_hbm,
     qkv_hbm,
     out_hbm,
+    table_hbm,
+    perm_in_hbm,
+    perm_query_hbm,
+    perm_out_hbm,
+    pick0_hbm,
+    pick1_hbm,
+    marks_hbm,
+    result_ref,
+    raw_ref,
+    gain_ref,
+    qkv_ref,
+    out_ref,
     table_ref,
     perm_in_ref,
     perm_query_ref,
@@ -217,11 +229,7 @@
     pick0_ref,
     pick1_ref,
     marks_ref,
-    result_ref,
-    raw_ref,
     x_ref,
-    qkv_ref,
-    out_ref,
     padded,
     moved,
     bias0,
@@ -231,7 +239,7 @@
     frame,
     backs,
     home,
-    weight_sem,
+    load_sem,
     send_sem,
     recv_sem,
     back_send_sem,
@@ -244,19 +252,30 @@
     inner = lat_count - 1
     is_first = (inner - i) // inner
     is_last = i // inner
-    up, down = i - 1 + is_first, i + 1 - is_last
-
-    def fetched(block):
-        return (
-            pltpu.make_async_copy(qkv_hbm.at[block], qkv_ref.at[block], weight_sem.at[block]),
-            pltpu.make_async_copy(out_hbm.at[block], out_ref.at[block], weight_sem.at[2 + block]),
-        )
-
-    raw_copy = pltpu.make_async_copy(raw_hbm, raw_ref, weight_sem.at[4])
-    raw_copy.start()
-    for block in range(2):
-        for copy in fetched(block):
-            copy.start()
+    odd = lax.rem(i, 2)
+    partner = i + 1 - 2 * odd
+    at_seam = is_first + is_last
+    across = i - 1 + 2 * odd
+    across_or_here = across + is_first - is_last
+
+    loads = [
+        (raw_hbm, raw_ref),
+        (table_hbm, table_ref),
+        (pick0_hbm, pick0_ref),
+        (gain_hbm, gain_ref),
+        (perm_in_hbm, perm_in_ref),
+        (qkv_hbm.at[0], qkv_ref.at[0]),
+        (perm_out_hbm, perm_out_ref),
+        (out_hbm.at[0], out_ref.at[0]),
+        (pick1_hbm, pick1_ref),
+        (marks_hbm, marks_ref),
+        (perm_query_hbm, perm_query_ref),
+        (qkv_hbm.at[1], qkv_ref.at[1]),
+        (out_hbm.at[1], out_ref.at[1]),
+    ]
+    loads = [pltpu.make_async_copy(src, dst, load_sem.at[n]) for n, (src, dst) in enumerate(loads)]
+    for copy in loads:
+        copy.start()
 
     barrier = pltpu.get_barrier_semaphore()
 
@@ -265,78 +284,81 @@
 
     greet(i, west)
     greet(i, east)
-
-    @pl.when(i > 0)
+    for lon in (west, j, east):
+        greet(partner, lon)
+
+    @pl.when(at_seam == 0)
     def _():
         for lon in (west, j, east):
-            greet(i - 1, lon)
-
-    @pl.when(i < inner)
-    def _():
-        for lon in (west, j, east):
-            greet(i + 1, lon)
-
-    bias0[...] = offset_bias(table_ref[0], padded, moved, pick0_ref[...], False)
-
-    PIECES = ((slice(24, 40), slice(0, 16)), (slice(0, 24), slice(16, 40)))
+            greet(across, lon)
+
+    OUTER, INNER, STAY, GO = 0, 1, 0, 1
     E, W = 0, 1
-
-    def outward(piece, number, which, quad, to, lat, lon):
-        rows = PIECES[piece][which]
+    base = (2 * odd, 2 - 2 * odd)
+    is_mid = ((odd, 1 - odd), (1 - odd, odd))
+
+    def piece_rows(piece, half, kind):
+        mid = is_mid[half][kind]
+        if piece == 0:
+            return pl.ds(pl.multiple_of(24 * mid, 8), 16)
+        return pl.ds(pl.multiple_of(16 - 16 * mid, 8), 24)
+
+    def outward(piece, number, half, kind, lon, win, quad, to_lat, to_lon):
+        rows = piece_rows(piece, half, kind)
         return pltpu.make_async_remote_copy(
-            src_ref=mine.at[which, quad, rows],
-            dst_ref=frame.at[to[0], to[1], to[2], rows],
+            src_ref=mine.at[half, kind, lon, rows],
+            dst_ref=frame.at[half, win, quad, rows],
             send_sem=send_sem.at[piece, number],
-            recv_sem=recv_sem.at[piece, to[0] * 8 + to[1] * 4 + to[2]],
-            device_id=(lat, lon),
+            recv_sem=recv_sem.at[piece, half * 8 + win * 4 + quad],
+            device_id=(to_lat, to_lon),
             device_id_type=MESH,
         )
 
-    def always_out(piece):
-        top, bottom = is_first * (BW - TW), is_last * (BW - TW)
+    def sideways(piece, half):
+        go_quad = base[half]
+        to_lat = partner
+        if half == OUTER:
+            go_quad = base[half] + at_seam * (2 - 2 * base[half])
+            to_lat = across_or_here
+        first = 4 * half
         return [
-            outward(piece, 0, 0, TE, (is_first, W, TE + top), up, east),
-            outward(piece, 1, 0, TW, (is_first, E, TW + top), up, west),
-            outward(piece, 2, 1, BE, (1 - is_last, W, BE - bottom), down, east),
-            outward(piece, 3, 1, BW, (1 - is_last, E, BW - bottom), down, west),
-            outward(piece, 4, 0, BE, (0, W, BE), i, east),
-            outward(piece, 5, 0, BW, (0, E, BW), i, west),
-            outward(piece, 6, 1, TE, (1, W, TE), i, east),
-            outward(piece, 7, 1, TW, (1, E, TW), i, west),
+            outward(piece, first, half, GO, 0, E, go_quad, to_lat, west),
+            outward(piece, first + 1, half, GO, 1, W, go_quad + 1, to_lat, east),
+            outward(piece, first + 2, half, STAY, 0, E, base[half], i, west),
+            outward(piece, first + 3, half, STAY, 1, W, base[half] + 1, i, east),
         ]
 
-    def up_out(piece):
+    def straight(piece, half):
+        to_lat = partner if half == INNER else across
+        first = 8 + 2 * half
         return [
-            outward(piece, 8, 0, TE, (0, E, TE), i - 1, j),
-            outward(piece, 9, 0, TW, (0, W, TW), i - 1, j),
+            outward(piece, first, half, GO, 0, W, base[half], to_lat, j),
+            outward(piece, first + 1, half, GO, 1, E, base[half] + 1, to_lat, j),
         ]
 
-    def down_out(piece):
-        return [
-            outward(piece, 10, 1, BE, (1, E, BE), i + 1, j),
-            outward(piece, 11, 1, BW, (1, W, BW), i + 1, j),
-        ]
-
     def send(piece):
-        for copy in always_out(piece):
+        @pl.when(at_seam == 0)
+        def _():
+            for copy in straight(piece, OUTER):
+                copy.start()
+
+        for copy in sideways(piece, OUTER) + straight(piece, INNER) + sideways(piece, INNER):
             copy.start()
 
-        @pl.when(i > 0)
-        def _():
-            for copy in up_out(piece):
-                copy.start()
-
-        @pl.when(i < inner)
-        def _():
-            for copy in down_out(piece):
-                copy.start()
-
     def keep(which, quad, rows, value):
-        mine[which, quad, rows, :] = value
-        if quad in ((BW, BE), (TW, TE))[which]:
-            frame[which, E if quad in (TE, BE) else W, quad, rows, :] = value
-
-    raw_copy.wait()
+        upper = quad in (TW, TE)
+        half = odd if upper else 1 - odd
+        kind = STAY if upper == (which == 1) else GO
+        lon = quad % 2
+        mine[half, kind, lon, rows, :] = value
+        if kind == STAY:
+            frame[half, E if lon else W, quad, rows, :] = value
+
+    loads[1].wait()
+    loads[2].wait()
+    bias0[...] = offset_bias(table_ref[0], padded, moved, pick0_ref[...], False)
+
+    loads[0].wait()
     for quad in range(4):
         end = quad * QUAD + QUAD
         for w in range(2):
@@ -346,7 +368,7 @@
             pl.ds(first_row, 6, stride=16), :
         ]
 
-    for copy in fetched(0):
+    for copy in loads[3:8]:
         copy.wait()
     qkv = qkv_ref[0]
     normed = jnp.concatenate(
@@ -370,7 +392,7 @@
     for quad in range(4):
         keep(0, quad, slice(24, 40), quad_rows(lower, quad, 24, 40))
         keep(1, quad, slice(0, 16), quad_rows(lower, quad, 0, 16))
-    pl.semaphore_wait(barrier, 2 + 3 * (1 - is_first) + 3 * (1 - is_last))
+    pl.semaphore_wait(barrier, 8 - 3 * at_seam)
     send(0)
 
     upper = plain_window(1)
@@ -383,25 +405,27 @@
         keep(1, quad, slice(24, 40), quad_rows(upper, quad, 24, 40))
     send(1)
 
-    @pl.when(i == 0)
+    @pl.when(at_seam == 1)
     def _():
-        frame[1, E, BE] = mine[0, TE]
-        frame[1, W, BW] = mine[0, TW]
-
-    @pl.when(i == inner)
-    def _():
-        frame[0, E, TE] = mine[1, BE]
-        frame[0, W, TW] = mine[1, BW]
-
-    last = is_last.astype(jnp.float32)
-    first = is_first.astype(jnp.float32)
+        frame[OUTER, W, 2 - base[OUTER]] = mine[OUTER, GO, 0]
+        frame[OUTER, E, 3 - base[OUTER]] = mine[OUTER, GO, 1]
+
+    for copy in loads[8:10]:
+        copy.wait()
+    last, first, odd_part = (flag.astype(jnp.float32) for flag in (is_last, is_first, odd))
     offsets1[...] = offset_bias(table_ref[1], padded, moved, pick1_ref[...], True)
     levels, in_second = marks_ref[0], marks_ref[1] > 0.5
-    same = ((jnp.zeros((ROW, LANES), jnp.float32), last * levels), ((1 - first) * levels, levels))
-    cross = (jnp.full((ROW, LANES), last * EXCLUDED), levels + first * EXCLUDED)
-    for which in range(2):
-        bottom, top = same[which]
-        apart = cross[which]
+    split = odd_part * levels
+    kinds = (
+        (
+            ((1 - odd_part) * (1 - first)) * levels,
+            ((1 - odd_part) + last) * levels,
+            (1 - odd_part) * levels + (first + last) * EXCLUDED,
+        ),
+        (split, split, split),
+    )
+    for group in range(2):
+        bottom, top, apart = kinds[group]
         added = (
             (bottom, apart),
             (jnp.where(in_second, apart, bottom), jnp.where(in_second, top, apart)),
@@ -412,129 +436,113 @@
                 start = win * PAIRED + (4 - 2 * pair) * ROW
                 for strip in range(6):
                     rows = slice(start + strip * ROW, start + strip * ROW + ROW)
-                    bias1[which, win * 3 + pair, strip * ROW : strip * ROW + ROW, :] = (
+                    bias1[group, win * 3 + pair, strip * ROW : strip * ROW + ROW, :] = (
                         offsets1[rows, :] + added[pair][strip // 3]
                     )
 
-    def arrived(which, win, quad):
+    def arrived(half, kind, win, quad):
         for piece in range(2):
-            here = frame.at[which, win, quad, PIECES[piece][which]]
-            sem = recv_sem.at[piece, which * 8 + win * 4 + quad]
+            rows = piece_rows(piece, half, kind)
+            here = frame.at[half, win, quad, rows]
+            sem = recv_sem.at[piece, half * 8 + win * 4 + quad]
             pltpu.make_async_copy(here, here, sem).wait()
 
-    for which in range(2):
-        for win, quad in ((E, TW), (E, BW), (W, TE), (W, BE)):
-            arrived(which, win, quad)
-
-    @pl.when(i < inner)
-    def _():
-        arrived(0, E, TE)
-        arrived(0, W, TW)
-
-    @pl.when(i > 0)
-    def _():
-        arrived(1, E, BE)
-        arrived(1, W, BW)
-
-    for copy in fetched(1):
-        copy.wait()
-    qkv = qkv_ref[1]
-    normed = [
-        normalised(frame[which, win].reshape(ROWS, D), gain_ref[1:2, :])
-        for which in range(2)
-        for win in range(2)
-    ]
-    asking = jnp.concatenate(
-        [
-            rounded(dot(perm_query_ref[...], jnp.concatenate(normed[2 * which : 2 * which + 2], axis=0)))
-            for which in range(2)
-        ],
-        axis=0,
-    )
-    queries1 = dot(asking, qkv[:, :D])
-    normed = jnp.concatenate([rounded(dot(perm_in_ref[1], n)) for n in normed], axis=0)
-    keys1 = rounded(dot(normed, qkv[:, D : 2 * D]))
-    values1 = rounded(dot(normed, qkv[:, 2 * D :]))
-
-    def shifted_rows(which):
+    def come(group):
+        own, other = base[group], 2 - base[group]
+        arrived(group, STAY, E, own)
+        arrived(group, STAY, W, own + 1)
+        arrived(group, GO, E, other)
+        arrived(group, GO, W, other + 1)
+        if group == INNER:
+            arrived(group, GO, W, other)
+            arrived(group, GO, E, other + 1)
+        else:
+
+            @pl.when(at_seam == 0)
+            def _():
+                arrived(group, GO, W, other)
+                arrived(group, GO, E, other + 1)
+
+    def shifted_set(group):
+        normed = [normalised(frame[group, win].reshape(ROWS, D), gain_ref[1:2, :]) for win in range(2)]
+        asking = rounded(dot(perm_query_ref[...], jnp.concatenate(normed, axis=0)))
+        normed = jnp.concatenate([rounded(dot(perm_in_ref[1], n)) for n in normed], axis=0)
+        qkv = qkv_ref[1]
+        queries = dot(asking, qkv[:, :D])
+        keys = rounded(dot(normed, qkv[:, D : 2 * D]))
+        values = rounded(dot(normed, qkv[:, 2 * D :]))
+
         def bias_at(a, lanes):
-            return bias1[which, a - 6 * which, :, lanes]
+            return bias1[group, a, :, lanes]
 
         windows = []
         for win in range(2):
-            rows = slice((2 * which + win) * WIN, (2 * which + win) * WIN + WIN)
-            start = 6 * which + 3 * win
-            windows.append((keys1[rows], values1[rows], range(start, start + 3)))
-        mixed = attend(queries1, windows, bias_at)
-        result = projected(mixed, perm_out_ref[1], out_ref[1])
-        stay = ((BW, BE), (TW, TE))[which]
+            rows = slice(win * WIN, win * WIN + WIN)
+            windows.append((keys[rows], values[rows], range(3 * win, 3 * win + 3)))
+        result = projected(attend(queries, windows, bias_at), perm_out_ref[1], out_ref[1])
         for quad in range(4):
-            state = frame[which, E if quad in (TE, BE) else W, quad]
-            value = state + quad_rows(result, quad, 0, QUAD)
-            if quad in stay:
-                home[which, quad] = value
-            else:
-                backs[which, quad % 2] = value
-
-    def backward(which, lat):
-        place = slice(0, 2) if which == 0 else slice(2, 4)
+            value = frame[group, E if quad % 2 else W, quad] + quad_rows(result, quad, 0, QUAD)
+            backs[group, quad // 2, quad % 2] = value
+
+    def backward(group):
+        other = 1 - base[group] // 2
         return pltpu.make_async_remote_copy(
-            src_ref=backs.at[which],
-            dst_ref=home.at[which, place],
-            send_sem=back_send_sem.at[which],
-            recv_sem=back_recv_sem.at[which],
-            device_id=(lat, j),
+            src_ref=backs.at[group, other],
+            dst_ref=home.at[group, GO],
+            send_sem=back_send_sem.at[group],
+            recv_sem=back_recv_sem.at[group],
+            device_id=(across if group == OUTER else partner, j),
             device_id_type=MESH,
         )
 
-    shifted_rows(0)
-
-    @pl.when(i < inner)
+    come(OUTER)
+    for copy in loads[10:]:
+        copy.wait()
+    shifted_set(OUTER)
+
+    @pl.when(at_seam == 0)
     def _():
-        backward(0, i + 1).start()
-
-    @pl.when(i == inner)
+        backward(OUTER).start()
+
+    @pl.when(at_seam == 1)
     def _():
-        home[1, 2:4] = backs[0]
-
-    shifted_rows(1)
-
-    @pl.when(i > 0)
+        home[OUTER, GO] = backs[OUTER, 1 - odd]
+
+    come(INNER)
+    shifted_set(INNER)
+    backward(INNER).start()
+    home[OUTER, STAY] = backs[OUTER, odd]
+    home[INNER, STAY] = backs[INNER, 1 - odd]
+
+    @pl.when(at_seam == 0)
     def _():
-        backward(1, i - 1).start()
-
-    @pl.when(i == 0)
-    def _():
-        home[0, 0:2] = backs[1]
-
-    @pl.when(i > 0)
-    def _():
-        backward(0, i - 1).wait_recv()
-
-    @pl.when(i < inner)
-    def _():
-        backward(1, i + 1).wait_recv()
+        backward(OUTER).wait_recv()
+
+    backward(INNER).wait_recv()
 
     for first_row, w, place, tile in strips():
         quad, row = place // QUAD, place % QUAD
-        which = 1 if (w == 0) == (row < HALF) else 0
+        outer_levels = (w == 0) == (row < HALF)
+        upper_half = quad in (TW, TE)
         result_ref[pl.ds(first_row, 6, stride=16), :] = home[
-            which, quad, row : row + 6, 128 * tile : 128 * tile + 128
+            odd if upper_half else 1 - odd,
+            STAY if upper_half == outer_levels else GO,
+            quad % 2,
+            row : row + 6,
+            128 * tile : 128 * tile + 128,
         ]
 
     for piece in range(2):
-        for copy in always_out(piece):
+        for copy in sideways(piece, OUTER) + straight(piece, INNER) + sideways(piece, INNER):
             copy.wait_send()
-
-    @pl.when(i > 0)
+    backward(INNER).wait_send()
+
+    @pl.when(at_seam == 0)
     def _():
-        for copy in up_out(0) + up_out(1) + [backward(1, i - 1)]:
-            copy.wait_send()
-
-    @pl.when(i < inner)
-    def _():
-        for copy in down_out(0) + down_out(1) + [backward(0, i + 1)]:
-            copy.wait_send()
+        for piece in range(2):
+            for copy in straight(piece, OUTER):
+                copy.wait_send()
+        backward(OUTER).wait_send()
 
 
 def shards(lat_count, lon_count, atmosphere, norm_gain, qkv_weight, out_weight, position_bias):
@@ -542,27 +550,25 @@
     x = x.transpose(0, 1, 3, 2, 4).reshape(1152, 128)
     operands = [x, norm_gain, qkv_weight, out_weight, position_bias]
     operands += [jnp.asarray(c) for c in CONSTANTS]
-    vmem, anywhere = pl.BlockSpec(memory_space=pltpu.VMEM), pl.BlockSpec(memory_space=pl.ANY)
+    quads = pltpu.VMEM((2, 2, 2, QUAD, D), jnp.float32)
     result = pl.pallas_call(
         functools.partial(kernel, lat_count, lon_count),
         out_shape=jax.ShapeDtypeStruct((1152, 128), jnp.float32),
-        in_specs=[anywhere, vmem, anywhere, anywhere] + [vmem] * (len(operands) - 4),
-        out_specs=vmem,
-        scratch_shapes=[
-            pltpu.VMEM((1152, 128), jnp.float32),
+        in_specs=[pl.BlockSpec(memory_space=pl.ANY)] * len(operands),
+        out_specs=pl.BlockSpec(memory_space=pltpu.VMEM),
+        scratch_shapes=[pltpu.VMEM(value.shape, value.dtype) for value in operands]
+        + [
             pltpu.VMEM((2, ROWS, D), jnp.float32),
-            pltpu.VMEM((2, D, 3 * D), jnp.bfloat16),
-            pltpu.VMEM((2, D, D), jnp.bfloat16),
             pltpu.VMEM((HEADS, 768), jnp.float32),
             pltpu.VMEM((LANES, 512), jnp.float32),
             pltpu.VMEM((OFFSETS, LANES), jnp.float32),
             pltpu.VMEM((2 * PAIRED, LANES), jnp.float32),
             pltpu.VMEM((2, 6, WIN, LANES), jnp.float32),
-            pltpu.VMEM((2, 4, QUAD, D), jnp.float32),
+            quads,
             pltpu.VMEM((2, 2, 4, QUAD, D), jnp.float32),
-            pltpu.VMEM((2, 2, QUAD, D), jnp.float32),
-            pltpu.VMEM((2, 4, QUAD, D), jnp.float32),
-            pltpu.SemaphoreType.DMA((5,)),
+            quads,
+            quads,
+            pltpu.SemaphoreType.DMA((len(operands) + 2,)),
             pltpu.SemaphoreType.DMA((2, 12)),
             pltpu.SemaphoreType.DMA((2, 16)),
             pltpu.SemaphoreType.DMA((2,)),

time: 34.7 us -> 30.8 us (0.89)
  Pallas kernels: 32.6 us -> 28.7 us
    pallas_call x1, Pallas kernels: 32.6 us -> 28.7 us  [shards(): pl.pallas_call(functools.partial(kernel, lat_count, lon_count), out_shape...]
where the time goes in v4:
time: 30.8 us; the launch traced here: 30.7 us
  Pallas kernels  28.7 us (93%)
  local copies, waits for them, and re-layouts  1.94 us (6%)
    pallas_call x1, Pallas kernels, shards(): pl.pallas_call(functools.partial(kernel, lat_count, lon_count), out_shape...  28.7 us
    unnamed x1, local copies, waits for them, and re-layouts  1.94 us

profile of v4, /device:TPU:1, one launch (start us, length us, event | category | flops | bytes accessed | tf_op | source)
XLA Modules:
  0.0 30.7 jit_solution(4530552317165000599)
XLA Ops:
  0.0 28.7 %shard_map.109 = f32[1152,128]{1,0:T(8,128)} custom-call(f32[1152,128]{1,0:T(8,128)} %bitcast.15, f32[2,512]{1,0:T(2,128)} %gain_hbm.1, bf16[2,512,1536]{2,1,0:T(8,128)(2,1)} %qkv_hbm.1, bf16[2,512,512]{2,1,0:T(8,128)(2,1)} %out_hbm.1, f32[2,16,759]{2,1,0:T(8,128)} %table_hbm.1, bf16[2,144,160]{2,1,0:T(8,128)(2,1)} %constant.12.clone.perm_in_hbm, ...), custom_call_target="tpu_custom_call" | custom-call | tf_op jit(solution)/shard_map/pallas_call | solution.py:554
  28.7 1.9 %copy.14 = f32[4,6,12,512]{3,0,2,1:T(4,128)} copy(f32[4,6,12,512]{3,0,2,1:T(4,128)} %bitcast.14) | data formatting | bytes 1179648

commit v5 on v4

--- a/solution.py
+++ b/solution.py
@@ -69,10 +69,32 @@
     lane = np.arange(LANES)[None, :]
     levels = np.where(np.arange(ROW)[:, None] // 12 == lane // 6 % 2, 0, EXCLUDED)
     second = np.broadcast_to(lane // 12 % 2, (ROW, LANES))
-    marks = np.stack([levels, second]).astype(np.float32)
-    return perm_in, perm_query, perm_out, pick0, pick1, marks
-
-
+    packed = np.zeros((PACKED_ROWS, 512), bf16)
+    for (row, col), part in (
+        (PICK0, pick0),
+        (PERM_IN[0], perm_in[0]),
+        (PERM_OUT[0], perm_out[0]),
+        (PICK1, pick1),
+        (PERM_IN[1], perm_in[1]),
+        (PERM_OUT[1], perm_out[1]),
+        (PERM_QUERY, perm_query),
+        (LEVELS, levels),
+        (SECOND, second),
+    ):
+        packed[row : row + part.shape[0], col : col + part.shape[1]] = part.astype(bf16)
+    return packed
+
+
+PICK0 = (0, 0)
+PERM_IN = ((272, 0), (912, 0))
+PERM_OUT = ((272, 256), (912, 256))
+FIRST_ROWS = 432
+PICK1 = (432, 0)
+PERM_QUERY = (1072, 0)
+LEVELS = (1216, 0)
+SECOND = (1248, 0)
+USED_ROWS = 1280
+PACKED_ROWS = 4096
 CONSTANTS = constants()
 
 
@@ -211,24 +233,14 @@
     qkv_hbm,
     out_hbm,
     table_hbm,
-    perm_in_hbm,
-    perm_query_hbm,
-    perm_out_hbm,
-    pick0_hbm,
-    pick1_hbm,
-    marks_hbm,
+    constant_hbm,
     result_ref,
     raw_ref,
     gain_ref,
     qkv_ref,
     out_ref,
     table_ref,
-    perm_in_ref,
-    perm_query_ref,
-    perm_out_ref,
-    pick0_ref,
-    pick1_ref,
-    marks_ref,
+    constant_ref,
     x_ref,
     padded,
     moved,
@@ -258,39 +270,39 @@
     across = i - 1 + 2 * odd
     across_or_here = across + is_first - is_last
 
+    barrier = pltpu.get_barrier_semaphore()
+
+    def greet(lat, lon):
+        pl.semaphore_signal(barrier, inc=1, device_id=(lat, lon), device_id_type=MESH)
+
+    @pl.when(at_seam == 0)
+    def _():
+        for lon in (west, east, j):
+            greet(across, lon)
+
+    greet(i, west)
+    greet(i, east)
+    for lon in (west, east, j):
+        greet(partner, lon)
+
+    def constant(place, rows, columns):
+        return constant_ref[place[0] : place[0] + rows, place[1] : place[1] + columns]
+
+    early, later = slice(0, FIRST_ROWS), slice(FIRST_ROWS, USED_ROWS)
     loads = [
         (raw_hbm, raw_ref),
         (table_hbm, table_ref),
-        (pick0_hbm, pick0_ref),
+        (constant_hbm.at[early], constant_ref.at[early]),
         (gain_hbm, gain_ref),
-        (perm_in_hbm, perm_in_ref),
         (qkv_hbm.at[0], qkv_ref.at[0]),
-        (perm_out_hbm, perm_out_ref),
         (out_hbm.at[0], out_ref.at[0]),
-        (pick1_hbm, pick1_ref),
-        (marks_hbm, marks_ref),
-        (perm_query_hbm, perm_query_ref),
+        (constant_hbm.at[later], constant_ref.at[later]),
         (qkv_hbm.at[1], qkv_ref.at[1]),
         (out_hbm.at[1], out_ref.at[1]),
     ]
     loads = [pltpu.make_async_copy(src, dst, load_sem.at[n]) for n, (src, dst) in enumerate(loads)]
-    for copy in loads:
+    for copy in loads[:6]:
         copy.start()
-
-    barrier = pltpu.get_barrier_semaphore()
-
-    def greet(lat, lon):
-        pl.semaphore_signal(barrier, inc=1, device_id=(lat, lon), device_id_type=MESH)
-
-    greet(i, west)
-    greet(i, east)
-    for lon in (west, j, east):
-        greet(partner, lon)
-
-    @pl.when(at_seam == 0)
-    def _():
-        for lon in (west, j, east):
-            greet(across, lon)
 
     OUTER, INNER, STAY, GO = 0, 1, 0, 1
     E, W = 0, 1
@@ -342,8 +354,11 @@
             for copy in straight(piece, OUTER):
                 copy.start()
 
-        for copy in sideways(piece, OUTER) + straight(piece, INNER) + sideways(piece, INNER):
+        for copy in sideways(piece, OUTER) + straight(piece, INNER):
             copy.start()
+        if piece == 1:
+            for copy in sideways(0, INNER) + sideways(1, INNER):
+                copy.start()
 
     def keep(which, quad, rows, value):
         upper = quad in (TW, TE)
@@ -356,7 +371,9 @@
 
     loads[1].wait()
     loads[2].wait()
-    bias0[...] = offset_bias(table_ref[0], padded, moved, pick0_ref[...], False)
+    bias0[...] = offset_bias(
+        table_ref[0], padded, moved, constant(PICK0, OFFSETS, 512), False
+    )
 
     loads[0].wait()
     for quad in range(4):
@@ -368,11 +385,14 @@
             pl.ds(first_row, 6, stride=16), :
         ]
 
-    for copy in loads[3:8]:
+    for copy in loads[3:6]:
         copy.wait()
+    for copy in loads[6:]:
+        copy.start()
     qkv = qkv_ref[0]
+    perm_in = constant(PERM_IN[0], WIN, ROWS)
     normed = jnp.concatenate(
-        [rounded(dot(perm_in_ref[0], normalised(x_ref[w], gain_ref[0:1, :]))) for w in range(2)], axis=0
+        [rounded(dot(perm_in, normalised(x_ref[w], gain_ref[0:1, :]))) for w in range(2)], axis=0
     )
     queries0 = dot(normed, qkv[:, :D])
     keys0 = rounded(dot(normed, qkv[:, D : 2 * D]))
@@ -386,7 +406,7 @@
         rows = slice(w * WIN, w * WIN + WIN)
         window = (keys0[rows], values0[rows], range(6 * w, 6 * w + 6))
         mixed = attend(queries0, [window], bias_at)
-        return x_ref[w] + projected(mixed, perm_out_ref[0], out_ref[0])
+        return x_ref[w] + projected(mixed, constant(PERM_OUT[0], ROWS, WIN), out_ref[0])
 
     lower = plain_window(0)
     for quad in range(4):
@@ -410,11 +430,13 @@
         frame[OUTER, W, 2 - base[OUTER]] = mine[OUTER, GO, 0]
         frame[OUTER, E, 3 - base[OUTER]] = mine[OUTER, GO, 1]
 
-    for copy in loads[8:10]:
-        copy.wait()
+    loads[6].wait()
     last, first, odd_part = (flag.astype(jnp.float32) for flag in (is_last, is_first, odd))
-    offsets1[...] = offset_bias(table_ref[1], padded, moved, pick1_ref[...], True)
-    levels, in_second = marks_ref[0], marks_ref[1] > 0.5
+    offsets1[...] = offset_bias(
+        table_ref[1], padded, moved, constant(PICK1, 2 * PAIRED, 512), True
+    )
+    levels = constant(LEVELS, 32, LANES).astype(jnp.float32)[:ROW]
+    in_second = constant(SECOND, 32, LANES).astype(jnp.float32)[:ROW] > 0.5
     split = odd_part * levels
     kinds = (
         (
@@ -465,8 +487,10 @@
 
     def shifted_set(group):
         normed = [normalised(frame[group, win].reshape(ROWS, D), gain_ref[1:2, :]) for win in range(2)]
-        asking = rounded(dot(perm_query_ref[...], jnp.concatenate(normed, axis=0)))
-        normed = jnp.concatenate([rounded(dot(perm_in_ref[1], n)) for n in normed], axis=0)
+        asking = constant(PERM_QUERY, WIN, 2 * ROWS)
+        asking = rounded(dot(asking, jnp.concatenate(normed, axis=0)))
+        perm_in = constant(PERM_IN[1], WIN, ROWS)
+        normed = jnp.concatenate([rounded(dot(perm_in, n)) for n in normed], axis=0)
         qkv = qkv_ref[1]
         queries = dot(asking, qkv[:, :D])
         keys = rounded(dot(normed, qkv[:, D : 2 * D]))
@@ -479,7 +503,8 @@
         for win in range(2):
             rows = slice(win * WIN, win * WIN + WIN)
             windows.append((keys[rows], values[rows], range(3 * win, 3 * win + 3)))
-        result = projected(attend(queries, windows, bias_at), perm_out_ref[1], out_ref[1])
+        perm_out = constant(PERM_OUT[1], ROWS, WIN)
+        result = projected(attend(queries, windows, bias_at), perm_out, out_ref[1])
         for quad in range(4):
             value = frame[group, E if quad % 2 else W, quad] + quad_rows(result, quad, 0, QUAD)
             backs[group, quad // 2, quad % 2] = value
@@ -496,7 +521,7 @@
         )
 
     come(OUTER)
-    for copy in loads[10:]:
+    for copy in loads[7:]:
         copy.wait()
     shifted_set(OUTER)
 
@@ -548,16 +573,16 @@
 def shards(lat_count, lon_count, atmosphere, norm_gain, qkv_weight, out_weight, position_bias):
     x = atmosphere.transpose(1, 2, 0, 3).reshape(6, 12, 4, 4, 128)
     x = x.transpose(0, 1, 3, 2, 4).reshape(1152, 128)
-    operands = [x, norm_gain, qkv_weight, out_weight, position_bias]
-    operands += [jnp.asarray(c) for c in CONSTANTS]
+    operands = [x, norm_gain, qkv_weight, out_weight, position_bias, jnp.asarray(CONSTANTS)]
     quads = pltpu.VMEM((2, 2, 2, QUAD, D), jnp.float32)
     result = pl.pallas_call(
         functools.partial(kernel, lat_count, lon_count),
         out_shape=jax.ShapeDtypeStruct((1152, 128), jnp.float32),
         in_specs=[pl.BlockSpec(memory_space=pl.ANY)] * len(operands),
         out_specs=pl.BlockSpec(memory_space=pltpu.VMEM),
-        scratch_shapes=[pltpu.VMEM(value.shape, value.dtype) for value in operands]
+        scratch_shapes=[pltpu.VMEM(value.shape, value.dtype) for value in operands[:5]]
         + [
+            pltpu.VMEM((USED_ROWS, 512), jnp.bfloat16),
             pltpu.VMEM((2, ROWS, D), jnp.float32),
             pltpu.VMEM((HEADS, 768), jnp.float32),
             pltpu.VMEM((LANES, 512), jnp.float32),
@@ -568,14 +593,14 @@
             pltpu.VMEM((2, 2, 4, QUAD, D), jnp.float32),
             quads,
             quads,
-            pltpu.SemaphoreType.DMA((len(operands) + 2,)),
+            pltpu.SemaphoreType.DMA((9,)),
             pltpu.SemaphoreType.DMA((2, 12)),
             pltpu.SemaphoreType.DMA((2, 16)),
             pltpu.SemaphoreType.DMA((2,)),
             pltpu.SemaphoreType.DMA((2,)),
         ],
         compiler_params=pltpu.CompilerParams(
-            collective_id=0, has_side_effects=True, vmem_limit_bytes=60 * 1024 * 1024
+            collective_id=0, has_side_effects=True, vmem_limit_bytes=53 * 1024 * 1024
         ),
     )(*operands)
     result = result.reshape(6, 12, 4, 4, 128).transpose(0, 1, 3, 2, 4)

time: 30.8 us -> 28.9 us (0.938)
  Pallas kernels: 28.7 us -> 26.3 us
  local copies, waits for them, and re-layouts: 1.94 us -> 2.4 us
    pallas_call x1, Pallas kernels: 28.7 us -> 26.3 us  [shards(): pl.pallas_call(functools.partial(kernel, lat_count, lon_count), out_shape...]
    unnamed x1 -> x5, local copies, waits for them, and re-layouts: 1.94 us -> 2.4 us
where the time goes in v5:
time: 28.9 us; the launch traced here: 28.7 us
  Pallas kernels  26.3 us (91%)
  local copies, waits for them, and re-layouts  2.4 us (8%)
    pallas_call x1, Pallas kernels, shards(): pl.pallas_call(functools.partial(kernel, lat_count, lon_count), out_shape...  26.3 us
    unnamed x5, local copies, waits for them, and re-layouts  2.4 us

profile of v5, /device:TPU:1, one launch (start us, length us, event | category | flops | bytes accessed | tf_op | source)
XLA Modules:
  0.0 28.7 jit_solution(18143338221191049599)
XLA Ops:
  0.0 0.0 copy-start
  0.0 0.9 %copy-done = f32[2,16,759]{2,1,0:T(8,128)S(1)} copy-done((f32[2,16,759]{2,1,0:T(8,128)S(1)}, f32[2,16,759]{2,1,0:T(8,128)}, u32[]{:S(2)}) %copy-start) | copy-done | bytes 97176
  0.9 0.0 copy-start.1
  0.9 0.7 %copy-done.1 = f32[2,512]{1,0:T(2,128)S(1)} copy-done((f32[2,512]{1,0:T(2,128)S(1)}, f32[2,512]{1,0:T(2,128)}, u32[]{:S(2)}) %copy-start.1) | copy-done | bytes 4120
  1.6 26.3 %shard_map.64 = f32[1152,128]{1,0:T(8,128)S(1)} custom-call(f32[1152,128]{1,0:T(8,128)} %bitcast.15, f32[2,512]{1,0:T(2,128)S(1)} %copy-done.1, bf16[2,512,1536]{2,1,0:T(8,128)(2,1)} %qkv_hbm.1, bf16[2,512,512]{2,1,0:T(8,128)(2,1)} %out_hbm.1, f32[2,16,759]{2,1,0:T(8,128)S(1)} %copy-done, bf16[4096,512]{1,0:T(8,128)(2,1)} %constant.2.clone.constant_hbm), custom_call_target="tpu_custom_call" | custom-call | tf_op jit(solution)/shard_map/pallas_call | solution.py:578
  27.9 0.8 %copy.9 = f32[4,6,12,512]{3,0,2,1:T(4,128)} copy(f32[4,6,12,512]{3,0,2,1:T(4,128)S(1)} %bitcast.14) | data formatting | bytes 1179648
Async XLA Ops:
  0.0 0.9 %copy-start = (f32[2,16,759]{2,1,0:T(8,128)S(1)}, f32[2,16,759]{2,1,0:T(8,128)}, u32[]{:S(2)}) copy-start(f32[2,16,759]{2,1,0:T(8,128)} %table_hbm.1) | copy-start | bytes 291460
  0.9 0.7 %copy-start.1 = (f32[2,512]{1,0:T(2,128)S(1)}, f32[2,512]{1,0:T(2,128)}, u32[]{:S(2)}) copy-start(f32[2,512]{1,0:T(2,128)} %gain_hbm.1) | copy-start | bytes 12292

commit v6 on v5

--- a/solution.py
+++ b/solution.py
@@ -573,6 +573,9 @@
 def shards(lat_count, lon_count, atmosphere, norm_gain, qkv_weight, out_weight, position_bias):
     x = atmosphere.transpose(1, 2, 0, 3).reshape(6, 12, 4, 4, 128)
     x = x.transpose(0, 1, 3, 2, 4).reshape(1152, 128)
+    norm_gain, position_bias = (
+        pltpu.with_memory_space_constraint(value, pltpu.HBM) for value in (norm_gain, position_bias)
+    )
     operands = [x, norm_gain, qkv_weight, out_weight, position_bias, jnp.asarray(CONSTANTS)]
     quads = pltpu.VMEM((2, 2, 2, QUAD, D), jnp.float32)
     result = pl.pallas_call(

time: 28.9 us -> 27.2 us (0.941)
  local copies, waits for them, and re-layouts: 2.4 us -> 0.82 us
    unnamed x5 -> x1, local copies, waits for them, and re-layouts: 2.4 us -> 0.82 us
where the time goes in v6:
time: 27.2 us; the launch traced here: 27.1 us
  Pallas kernels  26.3 us (97%)
  local copies, waits for them, and re-layouts  0.82 us (3%)
    pallas_call x1, Pallas kernels, shards(): pl.pallas_call(functools.partial(kernel, lat_count, lon_count), out_shape...  26.3 us
    unnamed x1, local copies, waits for them, and re-layouts  0.82 us

profile of v6, /device:TPU:1, one launch (start us, length us, event | category | flops | bytes accessed | tf_op | source)
XLA Modules:
  0.0 27.1 jit_solution(14790149670638908331)
XLA Ops:
  0.0 26.3 %shard_map.64 = f32[1152,128]{1,0:T(8,128)S(1)} custom-call(f32[1152,128]{1,0:T(8,128)} %bitcast.15, f32[2,512]{1,0:T(2,128)} %gain_hbm.1, bf16[2,512,1536]{2,1,0:T(8,128)(2,1)} %qkv_hbm.1, bf16[2,512,512]{2,1,0:T(8,128)(2,1)} %out_hbm.1, f32[2,16,759]{2,1,0:T(8,128)} %table_hbm.1, bf16[4096,512]{1,0:T(8,128)(2,1)} %constant.2.clone.constant_hbm), custom_call_target="tpu_custom_call" | custom-call | tf_op jit(solution)/shard_map/pallas_call | solution.py:581
  26.3 0.8 %copy.9 = f32[4,6,12,512]{3,0,2,1:T(4,128)} copy(f32[4,6,12,512]{3,0,2,1:T(4,128)S(1)} %bitcast.14) | data formatting | bytes 1179648

commit v7 on v6

--- a/solution.py
+++ b/solution.py
@@ -68,7 +68,19 @@
     pick1 = (index[:, None] == np.arange(512)[None, :]).astype(bf16)
     lane = np.arange(LANES)[None, :]
     levels = np.where(np.arange(ROW)[:, None] // 12 == lane // 6 % 2, 0, EXCLUDED)
-    second = np.broadcast_to(lane // 12 % 2, (ROW, LANES))
+    asked = np.zeros((96, 2 * QUAD))
+    answered = np.zeros((2 * QUAD, 96))
+    for lon in range(2):
+        for lev in range(2):
+            for r in range(3):
+                for c in range(6):
+                    place = lon * QUAD + lev * HALF + r * 6 + c
+                    for unit in range(2):
+                        if 0 <= r - unit < 2:
+                            token = (1 - lon) * 48 + unit * ROW + (r - unit) * 12 + (1 - lev) * 6 + c
+                            asked[token, place] = 1
+                            if unit == (r == 2):
+                                answered[place, token] = 1
     packed = np.zeros((PACKED_ROWS, 512), bf16)
     for (row, col), part in (
         (PICK0, pick0),
@@ -78,8 +90,9 @@
         (PERM_IN[1], perm_in[1]),
         (PERM_OUT[1], perm_out[1]),
         (PERM_QUERY, perm_query),
+        (ASKED, asked),
+        (ANSWERED, answered),
         (LEVELS, levels),
-        (SECOND, second),
     ):
         packed[row : row + part.shape[0], col : col + part.shape[1]] = part.astype(bf16)
     return packed
@@ -91,8 +104,9 @@
 FIRST_ROWS = 432
 PICK1 = (432, 0)
 PERM_QUERY = (1072, 0)
+ASKED = (1072, 384)
+ANSWERED = (1168, 384)
 LEVELS = (1216, 0)
-SECOND = (1248, 0)
 USED_ROWS = 1280
 PACKED_ROWS = 4096
 CONSTANTS = constants()
@@ -268,7 +282,6 @@
     partner = i + 1 - 2 * odd
     at_seam = is_first + is_last
     across = i - 1 + 2 * odd
-    across_or_here = across + is_first - is_last
 
     barrier = pltpu.get_barrier_semaphore()
 
@@ -304,7 +317,7 @@
     for copy in loads[:6]:
         copy.start()
 
-    OUTER, INNER, STAY, GO = 0, 1, 0, 1
+    OUTER, INNER, STAY, GO, SHARED = 0, 1, 0, 1, 2
     E, W = 0, 1
     base = (2 * odd, 2 - 2 * odd)
     is_mid = ((odd, 1 - odd), (1 - odd, odd))
@@ -315,50 +328,58 @@
             return pl.ds(pl.multiple_of(24 * mid, 8), 16)
         return pl.ds(pl.multiple_of(16 - 16 * mid, 8), 24)
 
-    def outward(piece, number, half, kind, lon, win, quad, to_lat, to_lon):
+    def outward(piece, number, half, kind, lon, group, win, to_lat, to_lon):
         rows = piece_rows(piece, half, kind)
+        quad = base[half] + lon
         return pltpu.make_async_remote_copy(
             src_ref=mine.at[half, kind, lon, rows],
-            dst_ref=frame.at[half, win, quad, rows],
+            dst_ref=frame.at[group, win, quad, rows],
             send_sem=send_sem.at[piece, number],
-            recv_sem=recv_sem.at[piece, half * 8 + win * 4 + quad],
+            recv_sem=recv_sem.at[piece, group * 8 + win * 4 + quad],
             device_id=(to_lat, to_lon),
             device_id_type=MESH,
         )
 
-    def sideways(piece, half):
-        go_quad = base[half]
-        to_lat = partner
-        if half == OUTER:
-            go_quad = base[half] + at_seam * (2 - 2 * base[half])
-            to_lat = across_or_here
-        first = 4 * half
+    def outer_sideways(piece):
         return [
-            outward(piece, first, half, GO, 0, E, go_quad, to_lat, west),
-            outward(piece, first + 1, half, GO, 1, W, go_quad + 1, to_lat, east),
-            outward(piece, first + 2, half, STAY, 0, E, base[half], i, west),
-            outward(piece, first + 3, half, STAY, 1, W, base[half] + 1, i, east),
+            outward(piece, 2 * kind + lon, OUTER, kind, lon, kind, win, i, to)
+            for kind in range(2)
+            for lon, win, to in ((0, E, west), (1, W, east))
         ]
 
-    def straight(piece, half):
-        to_lat = partner if half == INNER else across
-        first = 8 + 2 * half
+    def outer_across(piece):
         return [
-            outward(piece, first, half, GO, 0, W, base[half], to_lat, j),
-            outward(piece, first + 1, half, GO, 1, E, base[half] + 1, to_lat, j),
+            outward(piece, first + 2 * kind + lon, OUTER, kind, lon, 1 - kind, win, across, to)
+            for first, kind, places in (
+                (4, 0, ((0, E, west), (1, W, east))),
+                (4, 1, ((0, E, west), (1, W, east))),
+                (8, 0, ((0, W, j), (1, E, j))),
+                (8, 1, ((0, W, j), (1, E, j))),
+            )
+            for lon, win, to in places
+        ]
+
+    def inner_sideways(piece):
+        return [
+            outward(piece, 12 + 2 * kind + lon, INNER, kind, lon, SHARED, win, lat, to)
+            for kind, lat in ((GO, partner), (STAY, i))
+            for lon, win, to in ((0, E, west), (1, W, east))
+        ]
+
+    def inner_straight(piece):
+        return [
+            outward(piece, 16 + lon, INNER, GO, lon, SHARED, win, partner, j)
+            for lon, win in ((0, W), (1, E))
         ]
 
     def send(piece):
         @pl.when(at_seam == 0)
         def _():
-            for copy in straight(piece, OUTER):
+            for copy in outer_across(piece):
                 copy.start()
 
-        for copy in sideways(piece, OUTER) + straight(piece, INNER):
+        for copy in inner_sideways(piece) + inner_straight(piece) + outer_sideways(piece):
             copy.start()
-        if piece == 1:
-            for copy in sideways(0, INNER) + sideways(1, INNER):
-                copy.start()
 
     def keep(which, quad, rows, value):
         upper = quad in (TW, TE)
@@ -366,8 +387,7 @@
         kind = STAY if upper == (which == 1) else GO
         lon = quad % 2
         mine[half, kind, lon, rows, :] = value
-        if kind == STAY:
-            frame[half, E if lon else W, quad, rows, :] = value
+        frame[2 * half + kind, E if lon else W, quad, rows, :] = value
 
     loads[1].wait()
     loads[2].wait()
@@ -427,123 +447,133 @@
 
     @pl.when(at_seam == 1)
     def _():
-        frame[OUTER, W, 2 - base[OUTER]] = mine[OUTER, GO, 0]
-        frame[OUTER, E, 3 - base[OUTER]] = mine[OUTER, GO, 1]
+        for kind in range(2):
+            for win in range(2):
+                for lon in range(2):
+                    frame[kind, win, 2 - base[OUTER] + lon] = jnp.zeros((QUAD, D), jnp.float32)
 
     loads[6].wait()
-    last, first, odd_part = (flag.astype(jnp.float32) for flag in (is_last, is_first, odd))
+    seam, odd_part = at_seam.astype(jnp.float32), odd.astype(jnp.float32)
     offsets1[...] = offset_bias(
         table_ref[1], padded, moved, constant(PICK1, 2 * PAIRED, 512), True
     )
     levels = constant(LEVELS, 32, LANES).astype(jnp.float32)[:ROW]
-    in_second = constant(SECOND, 32, LANES).astype(jnp.float32)[:ROW] > 0.5
     split = odd_part * levels
-    kinds = (
-        (
-            ((1 - odd_part) * (1 - first)) * levels,
-            ((1 - odd_part) + last) * levels,
-            (1 - odd_part) * levels + (first + last) * EXCLUDED,
-        ),
-        (split, split, split),
-    )
-    for group in range(2):
-        bottom, top, apart = kinds[group]
-        added = (
-            (bottom, apart),
-            (jnp.where(in_second, apart, bottom), jnp.where(in_second, top, apart)),
-            (apart, top),
-        )
+    for win in range(2):
+        for pair in range(3):
+            for strip in range(6):
+                start = win * PAIRED + (4 - 2 * pair + strip) * ROW
+                bias1[8 + win * 3 + pair, strip * ROW : strip * ROW + ROW, :] = (
+                    offsets1[start : start + ROW, :] + split
+                )
+    beyond = ((1 - odd_part) * seam * EXCLUDED, odd_part * seam * EXCLUDED)
+    for kind in range(2):
+        parted = (split if kind == GO else levels - split) + jnp.zeros((ROW, LANES), jnp.float32)
+        added = [parted + beyond[upper] for upper in range(2)]
         for win in range(2):
-            for pair in range(3):
-                start = win * PAIRED + (4 - 2 * pair) * ROW
+            for unit in range(2):
                 for strip in range(6):
-                    rows = slice(start + strip * ROW, start + strip * ROW + ROW)
-                    bias1[group, win * 3 + pair, strip * ROW : strip * ROW + ROW, :] = (
-                        offsets1[rows, :] + added[pair][strip // 3]
+                    start = win * PAIRED + (1 - unit + strip) * ROW
+                    rows = pl.ds(pl.multiple_of(start + 3 * ROW * odd, 8), ROW)
+                    bias1[4 * kind + 2 * win + unit, strip * ROW : strip * ROW + ROW, :] = (
+                        offsets1[rows, :] + added[strip // 3]
                     )
 
-    def arrived(half, kind, win, quad):
+    def arrived(group, half, kind, win, quad):
         for piece in range(2):
             rows = piece_rows(piece, half, kind)
-            here = frame.at[half, win, quad, rows]
-            sem = recv_sem.at[piece, half * 8 + win * 4 + quad]
+            here = frame.at[group, win, quad, rows]
+            sem = recv_sem.at[piece, group * 8 + win * 4 + quad]
             pltpu.make_async_copy(here, here, sem).wait()
 
-    def come(group):
-        own, other = base[group], 2 - base[group]
-        arrived(group, STAY, E, own)
-        arrived(group, STAY, W, own + 1)
-        arrived(group, GO, E, other)
-        arrived(group, GO, W, other + 1)
-        if group == INNER:
-            arrived(group, GO, W, other)
-            arrived(group, GO, E, other + 1)
-        else:
-
-            @pl.when(at_seam == 0)
-            def _():
-                arrived(group, GO, W, other)
-                arrived(group, GO, E, other + 1)
-
-    def shifted_set(group):
-        normed = [normalised(frame[group, win].reshape(ROWS, D), gain_ref[1:2, :]) for win in range(2)]
-        asking = constant(PERM_QUERY, WIN, 2 * ROWS)
-        asking = rounded(dot(asking, jnp.concatenate(normed, axis=0)))
+    def outer_come():
+        own, other = base[OUTER], 2 - base[OUTER]
+        for kind in range(2):
+            arrived(kind, OUTER, kind, E, own)
+            arrived(kind, OUTER, kind, W, own + 1)
+
+        @pl.when(at_seam == 0)
+        def _():
+            for kind in range(2):
+                for win in range(2):
+                    for lon in range(2):
+                        arrived(kind, OUTER, kind, win, other + lon)
+
+    def inner_come():
+        own, other = base[INNER], 2 - base[INNER]
+        arrived(SHARED, INNER, STAY, E, own)
+        arrived(SHARED, INNER, STAY, W, own + 1)
+        for win in range(2):
+            for lon in range(2):
+                arrived(SHARED, INNER, STAY, win, other + lon)
+
+    def keys_and_values(normed):
         perm_in = constant(PERM_IN[1], WIN, ROWS)
         normed = jnp.concatenate([rounded(dot(perm_in, n)) for n in normed], axis=0)
         qkv = qkv_ref[1]
-        queries = dot(asking, qkv[:, :D])
         keys = rounded(dot(normed, qkv[:, D : 2 * D]))
         values = rounded(dot(normed, qkv[:, 2 * D :]))
+        rows = [slice(start, start + WIN) for start in range(0, keys.shape[0], WIN)]
+        return [(keys[r], values[r]) for r in rows]
+
+    def frames_normed(group):
+        gain = gain_ref[1:2, :]
+        return [normalised(frame[group, win].reshape(ROWS, D), gain) for win in range(2)]
+
+    def outer_part():
+        pairs = keys_and_values(frames_normed(STAY) + frames_normed(GO))
+        states = [mine[OUTER, kind].reshape(2 * QUAD, D) for kind in range(2)]
+        asked, answered = constant(ASKED, 96, 2 * QUAD), constant(ANSWERED, 2 * QUAD, 96)
+        asking = [rounded(dot(asked, normalised(state, gain_ref[1:2, :]))) for state in states]
+        queries = dot(jnp.concatenate(asking, axis=0), qkv_ref[1][:, :D])
 
         def bias_at(a, lanes):
-            return bias1[group, a, :, lanes]
-
-        windows = []
-        for win in range(2):
-            rows = slice(win * WIN, win * WIN + WIN)
-            windows.append((keys[rows], values[rows], range(3 * win, 3 * win + 3)))
+            return bias1[a, :, lanes]
+
+        windows = [(*pair, range(2 * n, 2 * n + 2)) for n, pair in enumerate(pairs)]
+        mixed = rounded(attend(queries, windows, bias_at))
+        mixed = [rounded(dot(answered, mixed[96 * kind : 96 * kind + 96])) for kind in range(2)]
+        result = dot(jnp.concatenate(mixed, axis=0), out_ref[1])
+        for kind in range(2):
+            value = states[kind] + result[2 * QUAD * kind : 2 * QUAD * (kind + 1)]
+            home[OUTER, kind] = value.reshape(2, QUAD, D)
+
+    def inner_part():
+        normed = frames_normed(SHARED)
+        pairs = keys_and_values(normed)
+        asking = constant(PERM_QUERY, WIN, 2 * ROWS)
+        asking = rounded(dot(asking, jnp.concatenate(normed, axis=0)))
+        queries = dot(asking, qkv_ref[1][:, :D])
+
+        def bias_at(a, lanes):
+            return bias1[8 + a, :, lanes]
+
+        windows = [(*pair, range(3 * n, 3 * n + 3)) for n, pair in enumerate(pairs)]
         perm_out = constant(PERM_OUT[1], ROWS, WIN)
         result = projected(attend(queries, windows, bias_at), perm_out, out_ref[1])
         for quad in range(4):
-            value = frame[group, E if quad % 2 else W, quad] + quad_rows(result, quad, 0, QUAD)
-            backs[group, quad // 2, quad % 2] = value
-
-    def backward(group):
-        other = 1 - base[group] // 2
+            value = frame[SHARED, E if quad % 2 else W, quad] + quad_rows(result, quad, 0, QUAD)
+            backs[quad // 2, quad % 2] = value
+
+    def backward():
         return pltpu.make_async_remote_copy(
-            src_ref=backs.at[group, other],
-            dst_ref=home.at[group, GO],
-            send_sem=back_send_sem.at[group],
-            recv_sem=back_recv_sem.at[group],
-            device_id=(across if group == OUTER else partner, j),
+            src_ref=backs.at[odd],
+            dst_ref=home.at[INNER, GO],
+            send_sem=back_send_sem.at[0],
+            recv_sem=back_recv_sem.at[0],
+            device_id=(partner, j),
             device_id_type=MESH,
         )
 
-    come(OUTER)
     for copy in loads[7:]:
         copy.wait()
-    shifted_set(OUTER)
-
-    @pl.when(at_seam == 0)
-    def _():
-        backward(OUTER).start()
-
-    @pl.when(at_seam == 1)
-    def _():
-        home[OUTER, GO] = backs[OUTER, 1 - odd]
-
-    come(INNER)
-    shifted_set(INNER)
-    backward(INNER).start()
-    home[OUTER, STAY] = backs[OUTER, odd]
-    home[INNER, STAY] = backs[INNER, 1 - odd]
-
-    @pl.when(at_seam == 0)
-    def _():
-        backward(OUTER).wait_recv()
-
-    backward(INNER).wait_recv()
+    inner_come()
+    inner_part()
+    backward().start()
+    outer_come()
+    outer_part()
+    home[INNER, STAY] = backs[1 - odd]
+    backward().wait_recv()
 
     for first_row, w, place, tile in strips():
         quad, row = place // QUAD, place % QUAD
@@ -558,16 +588,15 @@
         ]
 
     for piece in range(2):
-        for copy in sideways(piece, OUTER) + straight(piece, INNER) + sideways(piece, INNER):
+        for copy in outer_sideways(piece) + inner_straight(piece) + inner_sideways(piece):
             copy.wait_send()
-    backward(INNER).wait_send()
+    backward().wait_send()
 
     @pl.when(at_seam == 0)
     def _():
         for piece in range(2):
-            for copy in straight(piece, OUTER):
+            for copy in outer_across(piece):
                 copy.wait_send()
-        backward(OUTER).wait_send()
 
 
 def shards(lat_count, lon_count, atmosphere, norm_gain, qkv_weight, out_weight, position_bias):
@@ -591,16 +620,16 @@
             pltpu.VMEM((LANES, 512), jnp.float32),
             pltpu.VMEM((OFFSETS, LANES), jnp.float32),
             pltpu.VMEM((2 * PAIRED, LANES), jnp.float32),
-            pltpu.VMEM((2, 6, WIN, LANES), jnp.float32),
+            pltpu.VMEM((14, WIN, LANES), jnp.float32),
             quads,
-            pltpu.VMEM((2, 2, 4, QUAD, D), jnp.float32),
-            quads,
+            pltpu.VMEM((4, 2, 4, QUAD, D), jnp.float32),
+            pltpu.VMEM((2, 2, QUAD, D), jnp.float32),
             quads,
             pltpu.SemaphoreType.DMA((9,)),
-            pltpu.SemaphoreType.DMA((2, 12)),
-            pltpu.SemaphoreType.DMA((2, 16)),
-            pltpu.SemaphoreType.DMA((2,)),
-            pltpu.SemaphoreType.DMA((2,)),
+            pltpu.SemaphoreType.DMA((2, 18)),
+            pltpu.SemaphoreType.DMA((2, 24)),
+            pltpu.SemaphoreType.DMA((1,)),
+            pltpu.SemaphoreType.DMA((1,)),
         ],
         compiler_params=pltpu.CompilerParams(
             collective_id=0, has_side_effects=True, vmem_limit_bytes=53 * 1024 * 1024

time: 27.2 us -> 28.6 us (1.051)
  Pallas kernels: 26.3 us -> 27.7 us
    pallas_call x1, Pallas kernels: 26.3 us -> 27.7 us  [shards(): pl.pallas_call(functools.partial(kernel, lat_count, lon_count), out_shape...]
where the time goes in v7:
time: 28.6 us; the launch traced here: 28.5 us
  Pallas kernels  27.7 us (97%)
  local copies, waits for them, and re-layouts  0.82 us (3%)
    pallas_call x1, Pallas kernels, shards(): pl.pallas_call(functools.partial(kernel, lat_count, lon_count), out_shape...  27.7 us
    unnamed x1, local copies, waits for them, and re-layouts  0.82 us

profile of v7, /device:TPU:1, one launch (start us, length us, event | category | flops | bytes accessed | tf_op | source)
XLA Modules:
  0.0 28.5 jit_solution(4706203532347753689)
XLA Ops:
  0.0 27.7 %shard_map.64 = f32[1152,128]{1,0:T(8,128)S(1)} custom-call(f32[1152,128]{1,0:T(8,128)} %bitcast.15, f32[2,512]{1,0:T(2,128)} %gain_hbm.1, bf16[2,512,1536]{2,1,0:T(8,128)(2,1)} %qkv_hbm.1, bf16[2,512,512]{2,1,0:T(8,128)(2,1)} %out_hbm.1, f32[2,16,759]{2,1,0:T(8,128)} %table_hbm.1, bf16[4096,512]{1,0:T(8,128)(2,1)} %constant.2.clone.constant_hbm), custom_call_target="tpu_custom_call" | custom-call | tf_op jit(solution)/shard_map/pallas_call | solution.py:610
  27.7 0.8 %copy.9 = f32[4,6,12,512]{3,0,2,1:T(4,128)} copy(f32[4,6,12,512]{3,0,2,1:T(4,128)S(1)} %bitcast.14) | data formatting | bytes 1179648

commit v8 on v6

--- a/solution.py
+++ b/solution.py
@@ -354,9 +354,20 @@
             for copy in straight(piece, OUTER):
                 copy.start()
 
-        for copy in sideways(piece, OUTER) + straight(piece, INNER):
+        @pl.when(at_seam == 0)
+        def _():
+            for copy in sideways(piece, OUTER):
+                copy.start()
+
+        for copy in straight(piece, INNER):
             copy.start()
         if piece == 1:
+
+            @pl.when(at_seam == 1)
+            def _():
+                for copy in sideways(0, OUTER) + sideways(1, OUTER):
+                    copy.start()
+
             for copy in sideways(0, INNER) + sideways(1, INNER):
                 copy.start()
 

time: 27.2 us -> 27.3 us (level)
  no operation moved by 1% of the time
where the time goes in v8:
time: 27.3 us; the launch traced here: 27.2 us
  Pallas kernels  26.4 us (97%)
  local copies, waits for them, and re-layouts  0.82 us (3%)
    pallas_call x1, Pallas kernels, shards(): pl.pallas_call(functools.partial(kernel, lat_count, lon_count), out_shape...  26.4 us
    unnamed x1, local copies, waits for them, and re-layouts  0.82 us

profile of v8, /device:TPU:1, one launch (start us, length us, event | category | flops | bytes accessed | tf_op | source)
XLA Modules:
  0.0 27.2 jit_solution(4359652901257227681)
XLA Ops:
  0.0 26.4 %shard_map.64 = f32[1152,128]{1,0:T(8,128)S(1)} custom-call(f32[1152,128]{1,0:T(8,128)} %bitcast.15, f32[2,512]{1,0:T(2,128)} %gain_hbm.1, bf16[2,512,1536]{2,1,0:T(8,128)(2,1)} %qkv_hbm.1, bf16[2,512,512]{2,1,0:T(8,128)(2,1)} %out_hbm.1, f32[2,16,759]{2,1,0:T(8,128)} %table_hbm.1, bf16[4096,512]{1,0:T(8,128)(2,1)} %constant.2.clone.constant_hbm), custom_call_target="tpu_custom_call" | custom-call | tf_op jit(solution)/shard_map/pallas_call | solution.py:592
  26.4 0.8 %copy.9 = f32[4,6,12,512]{3,0,2,1:T(4,128)} copy(f32[4,6,12,512]{3,0,2,1:T(4,128)S(1)} %bitcast.14) | data formatting | bytes 1179648

commit v9 on v8

--- a/solution.py
+++ b/solution.py
@@ -496,7 +496,7 @@
                 arrived(group, GO, W, other)
                 arrived(group, GO, E, other + 1)
 
-    def shifted_set(group):
+    def shifted_set(group, give_back):
         normed = [normalised(frame[group, win].reshape(ROWS, D), gain_ref[1:2, :]) for win in range(2)]
         asking = constant(PERM_QUERY, WIN, 2 * ROWS)
         asking = rounded(dot(asking, jnp.concatenate(normed, axis=0)))
@@ -514,11 +514,21 @@
         for win in range(2):
             rows = slice(win * WIN, win * WIN + WIN)
             windows.append((keys[rows], values[rows], range(3 * win, 3 * win + 3)))
-        perm_out = constant(PERM_OUT[1], ROWS, WIN)
-        result = projected(attend(queries, windows, bias_at), perm_out, out_ref[1])
-        for quad in range(4):
-            value = frame[group, E if quad % 2 else W, quad] + quad_rows(result, quad, 0, QUAD)
-            backs[group, quad // 2, quad % 2] = value
+        mixed = rounded(attend(queries, windows, bias_at))
+        own = odd if group == OUTER else 1 - odd
+        for half in (1 - own, own):
+            rows = pl.ds(pl.multiple_of(PERM_OUT[1][0] + 2 * QUAD * half, 16), 2 * QUAD)
+            perm_out = constant_ref[rows, PERM_OUT[1][1] : PERM_OUT[1][1] + WIN]
+            result = dot(rounded(dot(perm_out, mixed)), out_ref[1])
+            for lon in range(2):
+                value = frame[group, E if lon else W, 2 * half + lon]
+                value = value + result[QUAD * lon : QUAD * lon + QUAD]
+                if half is own:
+                    home[group, STAY, lon] = value
+                else:
+                    backs[group, half, lon] = value
+            if half is not own:
+                give_back(group)
 
     def backward(group):
         other = 1 - base[group] // 2
@@ -534,21 +544,22 @@
     come(OUTER)
     for copy in loads[7:]:
         copy.wait()
-    shifted_set(OUTER)
-
-    @pl.when(at_seam == 0)
-    def _():
-        backward(OUTER).start()
-
-    @pl.when(at_seam == 1)
-    def _():
-        home[OUTER, GO] = backs[OUTER, 1 - odd]
-
+    def give_back(group):
+        if group == INNER:
+            backward(INNER).start()
+            return
+
+        @pl.when(at_seam == 0)
+        def _():
+            backward(OUTER).start()
+
+        @pl.when(at_seam == 1)
+        def _():
+            home[OUTER, GO] = backs[OUTER, 1 - odd]
+
+    shifted_set(OUTER, give_back)
     come(INNER)
-    shifted_set(INNER)
-    backward(INNER).start()
-    home[OUTER, STAY] = backs[OUTER, odd]
-    home[INNER, STAY] = backs[INNER, 1 - odd]
+    shifted_set(INNER, give_back)
 
     @pl.when(at_seam == 0)
     def _():

time: 27.3 us -> 27.3 us (level)
  no operation moved by 1% of the time
where the time goes in v9:
time: 27.3 us; the launch traced here: 27.2 us
  Pallas kernels  26.3 us (96%)
  local copies, waits for them, and re-layouts  0.82 us (3%)
    pallas_call x1, Pallas kernels, shards(): pl.pallas_call(functools.partial(kernel, lat_count, lon_count), out_shape...  26.3 us
    unnamed x1, local copies, waits for them, and re-layouts  0.82 us

profile of v9, /device:TPU:1, one launch (start us, length us, event | category | flops | bytes accessed | tf_op | source)
XLA Modules:
  0.0 27.2 jit_solution(16553343568075523468)
XLA Ops:
  0.0 26.3 %shard_map.64 = f32[1152,128]{1,0:T(8,128)S(1)} custom-call(f32[1152,128]{1,0:T(8,128)} %bitcast.15, f32[2,512]{1,0:T(2,128)} %gain_hbm.1, bf16[2,512,1536]{2,1,0:T(8,128)(2,1)} %qkv_hbm.1, bf16[2,512,512]{2,1,0:T(8,128)(2,1)} %out_hbm.1, f32[2,16,759]{2,1,0:T(8,128)} %table_hbm.1, bf16[4096,512]{1,0:T(8,128)(2,1)} %constant.2.clone.constant_hbm), custom_call_target="tpu_custom_call" | custom-call | tf_op jit(solution)/shard_map/pallas_call | solution.py:603
  26.3 0.8 %copy.9 = f32[4,6,12,512]{3,0,2,1:T(4,128)} copy(f32[4,6,12,512]{3,0,2,1:T(4,128)S(1)} %bitcast.14) | data formatting | bytes 1179648
